TPU v7x, 32 devices: a whole 2x2x4 slice. The times are simulated.
32 devices in a mesh: ctx: 4 (over x, core), exp: 8 (over z, y).
Axes of the slice: x: 2, y: 2, z: 4, core: 2. Of those that a mesh axis runs over, the one named last changes fastest.
Arguments:
- tokens: bfloat16 [8, 512, 1024], P('exp', 'ctx'), may hold values from -300 to 300, as said below
- expert_ids: int32 [8, 512, 2], P('exp', 'ctx'), may hold values from 0 to 7, all different within a row; in each aligned block of 128 rows (0 to 127, 128 to 255, ..., all dimensions but the last counted through in order) at most 48 rows name the same one
- attn_gain: float32 [1024], replicated, may hold values from 0.1 to 1.9
- w_query: bfloat16 [1024, 1024], P('exp'), may hold values from -0.1875 to 0.1875
- w_kv: bfloat16 [1024, 256], P('exp'), may hold values from -0.1875 to 0.1875
- w_out: bfloat16 [1024, 1024], P('exp'), may hold values from -0.1875 to 0.1875
- moe_gain: float32 [1024], replicated, may hold values from 0.1 to 1.9
- router: bfloat16 [1024, 8], replicated, may hold values from -0.375 to 0.375
- w_gate: bfloat16 [8, 1024, 4096], P('exp', None, 'ctx'), may hold values from -0.1875 to 0.1875
- w_up: bfloat16 [8, 1024, 4096], P('exp', None, 'ctx'), may hold values from -0.1875 to 0.1875
- w_down: bfloat16 [8, 4096, 1024], P('exp', 'ctx'), may hold values from -0.1875 to 0.1875
Outputs:
- attention_out: bfloat16 [8, 512, 1024], P('exp', 'ctx')
- expert_mix: bfloat16 [8, 512, 1024], P('exp', 'ctx')
Inputs may be any that keep to these rules, and one draw needn't show every extreme that they name: `expert_ids`: each row names 2 different experts. In the rows of one device (aligned blocks of 128 positions) no expert is named more than 48 times, a bound that some block reaches in every draw. `tokens`: each token and each feature carries its own scale.
All inputs are finite; a program needn't handle non-finite values.
Results may differ from a plain program's by a relative error of at most 0.018.
Values may be sent and summed in bfloat16 or wider, within the bound.
No kernel may reach another device: no remote copies, remote signals or barrier semaphores. Data moves between devices by JAX's collectives and lax.ppermute only.
A program may use at most 128 MiB of HBM per device.

v0:
```python
import jax
import jax.numpy as jnp
from jax import lax
from jax.sharding import PartitionSpec as P

HD = 128
TOP = 2


epsilon = 1e-06


def rms_scaled(values):
    return values * lax.rsqrt(jnp.mean(values * values, axis=-1, keepdims=True) + epsilon)


def body(
    tokens, expert_ids, attn_gain, w_query, w_kv, w_out, moe_gain, router, w_gate, w_up, w_down
):
    features = tokens.shape[-1]
    inputs = tokens.reshape(-1, features)
    tok_rows = inputs.shape[0]
    full_query, full_kv, full_out = (
        lax.all_gather(w_query, "exp", axis=0, tiled=True),
        lax.all_gather(w_kv, "exp", axis=0, tiled=True),
        lax.all_gather(w_out, "exp", axis=0, tiled=True),
    )
    floats = inputs.astype(jnp.float32)
    attn_in = (rms_scaled(floats) * attn_gain).astype(jnp.bfloat16)
    head_count = full_query.shape[1] // HD
    queries = jnp.dot(attn_in, full_query, preferred_element_type=jnp.float32).reshape(
        tok_rows, head_count, HD
    )
    queries = rms_scaled(queries).astype(jnp.bfloat16).reshape(tok_rows * head_count, HD)
    key_value = jnp.dot(attn_in, full_kv, preferred_element_type=jnp.float32)
    keys = rms_scaled(key_value[:, :HD]).astype(jnp.bfloat16)
    values = key_value[:, HD:].astype(jnp.bfloat16)
    score_scale = HD ** (-0.5)
    key_piece = lax.all_gather(keys, "ctx", axis=0, tiled=True)
    value_piece = lax.all_gather(values, "ctx", axis=0, tiled=True)
    scores = (
        lax.dot_general(
            queries, key_piece, (((1,), (1,)), ((), ())), preferred_element_type=jnp.float32
        )
        * score_scale
    )
    weights = jnp.exp(scores).astype(jnp.bfloat16)
    weighted = jnp.dot(weights, value_piece, preferred_element_type=jnp.float32)
    totals = jnp.sum(weights.astype(jnp.float32), axis=1)
    weighted, totals = (weighted, totals)
    context = (weighted / totals[:, None]).astype(jnp.bfloat16).reshape(tok_rows, head_count * HD)
    attention_out = jnp.dot(context, full_out, preferred_element_type=jnp.float32).astype(
        jnp.bfloat16
    )
    mixed_in = floats + attention_out.astype(jnp.float32)
    moe_in = (rms_scaled(mixed_in) * moe_gain).astype(jnp.bfloat16)
    experts = router.shape[1]
    logits = jnp.dot(moe_in, router, preferred_element_type=jnp.float32)
    pair_ids = expert_ids.reshape(tok_rows, TOP)
    match = pair_ids[:, :, None] == jnp.arange(experts)[None, None, :]
    chosen = jnp.sum(jnp.where(match, logits[:, None, :], 0.0), axis=2)
    first = jax.nn.sigmoid(chosen[:, 0] - chosen[:, 1])
    gates = jnp.stack([first, 1.0 - first], axis=1)
    counts = match.reshape(tok_rows * TOP, experts).astype(jnp.int32)
    earlier = jnp.cumsum(counts, axis=0) - counts
    slot = jnp.sum(earlier * counts, axis=1)
    capacity = max(2, 3 * tok_rows * TOP // (2 * experts))
    position = slot * experts + pair_ids.reshape(-1)
    buffer = (
        jnp.zeros((capacity * experts, features), jnp.bfloat16)
        .at[position]
        .set(jnp.repeat(moe_in, TOP, axis=0))
    )
    received = lax.all_to_all(
        buffer.reshape(capacity, experts, features), "exp", split_axis=1, concat_axis=0, tiled=True
    )
    gathered = lax.all_gather(received, "ctx", axis=0, tiled=True)
    gated = jnp.einsum("red,edf->ref", gathered, w_gate, preferred_element_type=jnp.float32)
    lifted = jnp.einsum("red,edf->ref", gathered, w_up, preferred_element_type=jnp.float32)
    hidden = (jax.nn.silu(gated) * lifted).astype(jnp.bfloat16)
    summed = lax.psum_scatter(
        jnp.einsum("ref,efd->red", hidden, w_down, preferred_element_type=jnp.float32).astype(
            jnp.bfloat16
        ),
        "ctx",
        scatter_dimension=0,
        tiled=True,
    )
    returned = lax.all_to_all(summed, "exp", split_axis=0, concat_axis=1, tiled=True)
    picked = returned.reshape(capacity * experts, features)[position].reshape(
        tok_rows, TOP, features
    )
    expert_mix = jnp.sum(gates[:, :, None] * picked.astype(jnp.float32), axis=1).astype(
        jnp.bfloat16
    )
    return (attention_out.reshape(tokens.shape), expert_mix.reshape(tokens.shape))


def solution(mesh):
    in_specs = (
        P("exp", "ctx", None),
        P("exp", "ctx", None),
        P(),
        P("exp", None),
        P("exp", None),
        P("exp", None),
        P(),
        P(),
        P("exp", None, "ctx"),
        P("exp", None, "ctx"),
        P("exp", "ctx", None),
    )
    out_specs = (P("exp", "ctx", None), P("exp", "ctx", None))
    return jax.shard_map(body, mesh=mesh, in_specs=in_specs, out_specs=out_specs, check_vma=False)
```

profile of v0, /device:TPU:0, one launch (start us, length us, event | category | flops | bytes accessed | tf_op | source)
XLA Modules:
  0.0 276.5 jit_solution(11645384030405082887)
XLA Ops:
  11.9 34.2 %all_gather.19 = bf16[1024,256]{1,0:T(8,128)(2,1)S(1)} all-gather(bf16[128,256]{1,0:T(8,128)(2,1)} %param.15), channel_id=1, replica_groups=mesh['ctx'=4,'exp'=8] {'exp'}, dimensions={0}, use_global_device_ids=true | all-gather | bytes 589824 | tf_op jit(solution)/shard_map/all_gather | solution.py:25
  46.1 1.2 fusion.29
  47.3 5.4 %all_gather.21 = bf16[512,128]{1,0:T(8,128)(2,1)S(1)} all-gather(bf16[128,128]{1,0:T(8,128)(2,1)S(1)} %slice.36), channel_id=1, replica_groups=mesh['ctx'=4,'exp'=8] {'ctx'}, dimensions={0}, use_global_device_ids=true | all-gather | bytes 163840 | tf_op jit(solution)/shard_map/all_gather | solution.py:40
  53.0 5.4 %all_gather.20 = bf16[512,128]{1,0:T(8,128)(2,1)S(1)} all-gather(bf16[128,128]{1,0:T(8,128)(2,1)S(1)} %multiply_convert_fusion.2), channel_id=1, replica_groups=mesh['ctx'=4,'exp'=8] {'ctx'}, dimensions={0}, use_global_device_ids=true | all-gather | bytes 163840 | tf_op jit(solution)/shard_map/all_gather | solution.py:39
  58.5 5.2 %all-gather.4.cloned.1.call-done = bf16[1024,1024]{1,0:T(8,128)(2,1)} async-done(((bf16[128,1024]{1,0:T(8,128)(2,1)}), bf16[1024,1024]{1,0:T(8,128)(2,1)}) %all-gather.4.cloned.1.call-update) | async-done | bytes 2097168 | tf_op jit(solution)/shard_map/all_gather | solution.py:24
  63.7 4.0 %copy.56 = bf16[1024,1024]{1,0:T(8,128)(2,1)} copy(bf16[1024,1024]{0,1:T(8,128)(2,1)} %bitcast.134) | data formatting | bytes 4194304 | tf_op jit(solution)/shard_map/dot_general | solution.py:31
  67.7 2.5 multiply_reduce_fusion.2
  71.7 42.9 %all-gather.6.cloned.1.call-done = bf16[1024,1024]{1,0:T(8,128)(2,1)} async-done(((bf16[128,1024]{1,0:T(8,128)(2,1)}), bf16[1024,1024]{1,0:T(8,128)(2,1)}) %all-gather.6.cloned.1.call-update) | async-done | bytes 2097168 | tf_op jit(solution)/shard_map/all_gather | solution.py:26
  114.6 2.1 multiply_reduce_fusion.1
  118.1 2.4 scatter_custom_fusion
  121.0 23.1 %all_to_all.33 = bf16[48,8,1024]{2,0,1:T(8,128)(2,1)} all-to-all(bf16[48,8,1024]{2,0,1:T(8,128)(2,1)S(1)} %copy.62), channel_id=1, replica_groups=mesh['ctx'=4,'exp'=8] {'exp'}, dimensions={1} | all-to-all | bytes 1572864 | tf_op jit(solution)/shard_map/all_to_all | solution.py:74
  144.3 27.4 %all-gather.8.cloned.1.call-done = bf16[1536,1,1024]{2,0,1:T(8,128)(2,1)} async-done(((bf16[384,1,1024]{2,0,1:T(8,128)(2,1)}), bf16[1536,1,1024]{2,0,1:T(8,128)(2,1)}) %all-gather.8.cloned.1.call-update) | async-done | bytes 3145744 | tf_op jit(solution)/shard_map/all_gather | solution.py:77
  171.8 7.3 %fusion.7 = f32[1536,1024]{1,0:T(8,128)} fusion(bf16[1536,1,1024]{2,0,1:T(8,128)(2,1)} %all-gather.8.cloned.1.call-done, bf16[1,1024,1024]{2,1,0:T(8,128)(2,1)S(1)} %copy-done), kind=kOutput, calls=%fused_computation.13 | convolution fusion | flops 3221225472 | bytes 11534336 | tf_op jit(solution)/shard_map/red,edf->ref/dot_general | solution.py:78
  179.0 11.7 %fusion.4 = bf16[1536,1,1024]{2,0,1:T(8,128)(2,1)} fusion(f32[1536,1024]{1,0:T(8,128)} %fusion.7, bf16[1536,1,1024]{2,0,1:T(8,128)(2,1)} %all-gather.8.cloned.1.call-done, bf16[1,1024,1024]{2,1,0:T(8,128)(2,1)} %param.21, bf16[1,1024,1024]{2,1,0:T(8,128)(2,1)} %param.20), kind=kOutput, calls=%fused_computation.10 | convolution fusion | flops 6453460992 | bytes 16777216 | tf_op jit(solution)/shard_map/ref,efd->red/dot_general | solution.py:82
  190.7 38.1 %reduce-scatter.2.cloned.1.call-done = bf16[384,1,1024]{2,0,1:T(8,128)(2,1)} async-done(((bf16[1536,1,1024]{2,0,1:T(8,128)(2,1)}), bf16[384,1,1024]{2,0,1:T(8,128)(2,1)}) %reduce-scatter.2.cloned.1.call-update) | async-done | bytes 786448 | tf_op jit(solution)/shard_map/reduce_scatter | solution.py:81
  229.4 2.4 reduce.2
  231.7 1.4 reshape.191
  233.2 5.5 %all-to-all-start.1 = ((bf16[8,2,24576]{2,1,0:T(2,128)(2,1)}), bf16[8,2,24576]{2,1,0:T(2,128)(2,1)S(1)}, u32[]{:S(2)}, u32[]{:S(2)}) async-start(bf16[8,2,24576]{2,1,0:T(2,128)(2,1)} %reshape.191), calls=%async_computation.2 | async-start | bytes 1572864 | tf_op jit(solution)/shard_map/all_to_all | solution.py:89
  239.1 19.8 %all-to-all-done.1 = bf16[8,2,24576]{2,1,0:T(2,128)(2,1)S(1)} async-done(((bf16[8,2,24576]{2,1,0:T(2,128)(2,1)}), bf16[8,2,24576]{2,1,0:T(2,128)(2,1)S(1)}, u32[]{:S(2)}, u32[]{:S(2)}) %all-to-all-start.1) | async-done | bytes 786464 | tf_op jit(solution)/shard_map/all_to_all | solution.py:89
  258.9 3.2 %reshape.192 = bf16[384,1,1024]{2,1,0:T(2,128)(2,1)} reshape(bf16[8,2,24576]{2,1,0:T(2,128)(2,1)S(1)} %all-to-all-done.1) | data formatting | bytes 1572864
  262.1 1.7 copy.65
  264.2 2.0 gather_fusion
  266.1 1.7 reshape.170
  267.8 2.1 multiply_reduce_fusion
  (58 shorter events, 9.7 us)
Async XLA Ops:
  7.2 164.6 %copy-start = (bf16[1,1024,1024]{2,1,0:T(8,128)(2,1)S(1)}, bf16[1,1024,1024]{2,1,0:T(8,128)(2,1)}, u32[]{:S(2)}) copy-start(bf16[1,1024,1024]{2,1,0:T(8,128)(2,1)} %param.19) | copy-start | bytes 6291460
  7.2 56.5 %all-gather.4.cloned.1.call-start = ((), (), s32[]{:S(2)}) async-start(), calls=%async_computation.3 | async-start | bytes 2359296 | tf_op jit(solution)/shard_map/all_gather | solution.py:24
  7.9 106.7 %all-gather.6.cloned.1.call-start = ((), (), s32[]{:S(2)}) async-start(), calls=%async_computation.4 | async-start | bytes 2359296 | tf_op jit(solution)/shard_map/all_gather | solution.py:26
  8.7 163.1 %all-gather.8.cloned.1.call-start = ((), (), s32[]{:S(2)}) async-start(), calls=%async_computation.5 | async-start | bytes 3932160 | tf_op jit(solution)/shard_map/all_gather | solution.py:77
  63.7 4.0 %copy-start.1 = (bf16[1,128,1024]{2,1,0:T(8,128)(2,1)S(1)}, bf16[1,128,1024]{2,1,0:T(8,128)(2,1)}, u32[]{:S(2)}) copy-start(bf16[1,128,1024]{2,1,0:T(8,128)(2,1)} %param.11) | copy-start | bytes 786436
  63.7 4.0 %copy-start.3 = (f32[1024]{0:T(1024)S(1)}, f32[1024]{0:T(1024)}, u32[]{:S(2)}) copy-start(f32[1024]{0:T(1024)} %param.13) | copy-start | bytes 12292
  71.5 45.2 %copy-start.5 = (f32[1024]{0:T(1024)S(1)}, f32[1024]{0:T(1024)}, u32[]{:S(2)}) copy-start(f32[1024]{0:T(1024)} %param.17) | copy-start | bytes 12292
  116.7 4.3 %copy-start.2 = (bf16[128,1024]{1,0:T(8,128)(2,1)}, bf16[128,1024]{1,0:T(8,128)(2,1)S(1)}, u32[]{:S(2)}) copy-start(bf16[128,1024]{1,0:T(8,128)(2,1)S(1)} %get-tuple-element.9) | copy-start | bytes 786436
  144.1 84.7 %reduce-scatter.2.cloned.1.call-start = ((), (), s32[]{:S(2)}) async-start(), calls=%async_computation.6 | async-start | bytes 3932160 | tf_op jit(solution)/shard_map/reduce_scatter | solution.py:81
  229.4 9.4 %copy-start.4 = (bf16[1024,8]{0,1:T(8,128)(2,1)S(1)}, bf16[1024,8]{0,1:T(8,128)(2,1)}, u32[]{:S(2)}) copy-start(bf16[1024,8]{0,1:T(8,128)(2,1)} %param.18) | copy-start | bytes 49156
  231.7 7.2 %copy-start.6 = (s32[1,128,2]{1,2,0:T(2,128)S(1)}, s32[1,128,2]{1,2,0:T(2,128)}, u32[]{:S(2)}) copy-start(s32[1,128,2]{1,2,0:T(2,128)} %param.12) | copy-start | bytes 3076
  233.2 25.7 %all-to-all-start.1 = ((bf16[8,2,24576]{2,1,0:T(2,128)(2,1)}), bf16[8,2,24576]{2,1,0:T(2,128)(2,1)S(1)}, u32[]{:S(2)}, u32[]{:S(2)}) async-start(bf16[8,2,24576]{2,1,0:T(2,128)(2,1)} %reshape.191), calls=%async_computation.2 | async-start | bytes 1572864 | tf_op jit(solution)/shard_map/all_to_all | solution.py:89
Sparse Core Ops, SparseCore 0:
  10.1 53.5 all-gather.3
  65.8 48.7 all-gather.5
  144.2 27.5 all-gather.7
  190.8 37.9 reduce-scatter.1
where the time goes:
time: 277 us; the launch traced here: 276 us
  waiting for transfers between devices  135 us (49%)
  blocking collectives  68.1 us (25%)
  matrix products  26 us (9%)
  local copies, waits for them, and re-layouts  20.7 us (7%)
  between operations  14 us (5%)
  other arithmetic  6.86 us (2%)
  starting transfers between devices  5.85 us (2%)
    all_gather x1, waiting for transfers between devices, body(): lax.all_gather(w_out, 'exp', axis=0, tiled=True)  42.9 us
    reduce_scatter x1, waiting for transfers between devices, body(): lax.psum_scatter(jnp.einsum('ref,efd->red', hidden, w_down, preferred_ele...  38.1 us
    all_gather x1, blocking collectives, body(): lax.all_gather(w_kv, 'exp', axis=0, tiled=True)  34.2 us
    all_gather x1, waiting for transfers between devices, body(): gathered = lax.all_gather(received, 'ctx', axis=0, tiled=True)  27.4 us
    all_to_all x1, blocking collectives, body(): lax.all_to_all(buffer.reshape(capacity, experts, features), 'exp', split_...  23.1 us
    all_to_all x1, waiting for transfers between devices, body(): lax.all_to_all(summed, 'exp', split_axis=0, concat_axis=1, tiled=True)  19.8 us
    dot_general x1, matrix products, body(): jnp.einsum('ref,efd->red', hidden, w_down, preferred_element_type=jnp.flo...  11.7 us
    dot_general x1, matrix products, body(): jnp.einsum('red,edf->ref', gathered, w_gate, preferred_element_type=jnp.f...  7.25 us
  transfers between devices with their start and end apart: 5, of which 5 were waited for; matrix products, arithmetic and copies ran while one was open for 5% of the time, Pallas kernels for 0%

commit v1 on v0

v1 whole, which is shorter than its diff:
```python
import functools

import jax
import jax.numpy as jnp
from jax import lax
from jax.experimental import pallas as pl
from jax.experimental.pallas import tpu as pltpu
from jax.sharding import PartitionSpec as P

HD = 128
TOP = 2
EPSILON = 1e-06
F32 = jnp.float32
BF16 = jnp.bfloat16
VMEM = pl.BlockSpec(memory_space=pltpu.VMEM)
SMEM = pl.BlockSpec(memory_space=pltpu.SMEM)


def rms_scaled(values):
    return values * lax.rsqrt(jnp.mean(values * values, axis=-1, keepdims=True) + EPSILON)


def swap(value, axis, bits):
    size = lax.axis_size(axis)
    return lax.ppermute(value, axis, [(i, i ^ bits) for i in range(size)])


def call(kernel, outs, scratch, flops, args, specs=None):
    moved = sum(a.size * a.dtype.itemsize for a in args) + sum(
        o.size * o.dtype.itemsize for o in outs
    )
    return pl.pallas_call(
        kernel,
        out_shape=outs,
        in_specs=[SMEM] + [VMEM] * (len(args) - 1) if specs is None else specs,
        out_specs=[VMEM] * len(outs),
        scratch_shapes=scratch,
        cost_estimate=pl.CostEstimate(flops=flops, bytes_accessed=moved, transcendentals=0),
        compiler_params=pltpu.CompilerParams(vmem_limit_bytes=48 * 1024 * 1024),
    )(*args)


def shape(rows, columns, kind=BF16):
    return jax.ShapeDtypeStruct((rows, columns), kind)


def project_kernel(count, heads, place, *refs):
    rows, weights = refs[:4], refs[4 : 4 + count]
    q_ref, kv_ref, whole, attn = refs[4 + count :]
    me, core = place[0], place[1]
    depth = weights[0].shape[0]
    for k, piece in enumerate(weights):
        start = pl.multiple_of(jnp.bitwise_xor(me, k) * depth, depth)
        whole[pl.ds(start, depth), :] = piece[...]
    block = rows[0].shape[0]
    for j, piece in enumerate(rows):
        spot = (j // 2) * 2 + jnp.bitwise_xor(core, j % 2)
        attn[pl.ds(pl.multiple_of(spot * block, block), block), :] = piece[...]
    for j in range(4):
        at = pl.ds(j * block, block)
        made = jnp.dot(attn[at, :], whole[...], preferred_element_type=F32)
        for h in range(heads):
            columns = slice(h * HD, (h + 1) * HD)
            q_ref[at, columns] = rms_scaled(made[:, columns]).astype(BF16)
        last = made[:, heads * HD :]
        scale = lax.rsqrt(jnp.mean(last * last, axis=-1, keepdims=True) + EPSILON)
        kv_ref[at, :] = (last * jnp.where(core == 0, scale, 1.0)).astype(BF16)


def attend_kernel(heads, place, q_ref, mine_ref, other_ref, near_ref, far_ref):
    core = place[1]
    mine, other = mine_ref[...], other_ref[...]
    keys = jnp.where(core == 0, mine, other)
    values = jnp.where(core == 0, other, mine)
    half = near_ref.shape[0]
    for out, base in ((far_ref, half), (near_ref, 0)):
        for h in range(heads):
            columns = slice(h * HD, (h + 1) * HD)
            scores = lax.dot_general(
                q_ref[base : base + half, columns],
                keys,
                (((1,), (1,)), ((), ())),
                preferred_element_type=F32,
            ) * (HD**-0.5)
            weights = jnp.exp(scores).astype(BF16)
            weighted = jnp.dot(weights, values, preferred_element_type=F32)
            totals = jnp.sum(weights.astype(F32), axis=1, keepdims=True)
            out[:, columns] = (weighted / totals).astype(BF16)


def route_kernel(count, capacity, blocks, place, *refs):
    contexts, own, theirs = refs[:4], refs[4 : 4 + count], refs[4 + count : 4 + 2 * count]
    tokens, gain, router, ids = refs[4 + 2 * count : 8 + 2 * count]
    outs = refs[8 + 2 * count :]
    attention_out, route, buffers = outs[0], outs[1], outs[2 : 2 + blocks]
    whole, context, total = outs[2 + blocks :]
    me, core, ctx = place[0], place[1], place[2]
    depth, half = own[0].shape
    wide = contexts[0].shape[1]
    for k in range(count):
        at = pl.ds(pl.multiple_of(jnp.bitwise_xor(me, k) * depth, depth), depth)
        whole[0, at, :] = own[k][...]
        whole[1, at, :] = theirs[k][...]
    for j, piece in enumerate(contexts):
        start = pl.multiple_of(jnp.bitwise_xor(ctx, j) * wide, wide)
        context[:, pl.ds(start, wide)] = piece[...]
    for j in range(2):
        start = pl.multiple_of(jnp.bitwise_xor(core, j) * half, half)
        total[:, pl.ds(start, half)] = jnp.dot(
            context[...], whole[j], preferred_element_type=F32
        )
    out = total[...].astype(BF16)
    attention_out[...] = out
    mixed = tokens[...].astype(F32) + out.astype(F32)
    moe_in = (rms_scaled(mixed) * gain[...]).astype(BF16)
    logits = jnp.dot(moe_in, router[...], preferred_element_type=F32)
    rows, experts = logits.shape
    lane = lax.broadcasted_iota(jnp.int32, (rows, experts), 1)
    first, second = ids[:, 0:1], ids[:, 1:2]
    is_first, is_second = lane == first, lane == second
    chosen = [
        jnp.sum(jnp.where(m, logits, 0.0), axis=1, keepdims=True) for m in (is_first, is_second)
    ]
    named = (is_first | is_second).astype(F32).astype(BF16)
    before = lax.broadcasted_iota(jnp.int32, (rows, rows), 0) > lax.broadcasted_iota(
        jnp.int32, (rows, rows), 1
    )
    earlier = jnp.dot(
        before.astype(F32).astype(BF16), named, preferred_element_type=F32
    )
    slots = [
        jnp.sum(jnp.where(m, earlier, 0.0), axis=1, keepdims=True).astype(jnp.int32)
        for m in (is_first, is_second)
    ]
    spots = [
        jnp.bitwise_xor(e, me) * capacity + s for e, s in zip((first, second), slots)
    ]
    gate = 1.0 / (1.0 + jnp.exp(chosen[1] - chosen[0]))
    column = lax.broadcasted_iota(jnp.int32, route.shape, 1)
    route[...] = jnp.where(
        column == 0,
        spots[0].astype(F32),
        jnp.where(column == 1, spots[1].astype(F32), gate),
    )
    lines = sum(b.shape[0] for b in buffers)
    place_of = lax.broadcasted_iota(jnp.int32, (rows, lines), 1)
    pick = ((place_of == spots[0]) | (place_of == spots[1])).astype(F32).astype(BF16)
    routed = lax.dot_general(
        pick, moe_in, (((0,), (0,)), ((), ())), preferred_element_type=F32
    ).astype(BF16)
    start = 0
    for b in buffers:
        b[...] = routed[start : start + b.shape[0]]
        start += b.shape[0]


def expert_kernel(parts, *refs):
    rows, (w_gate, w_up, w_down) = refs[:parts], refs[parts : parts + 3]
    outs, (joined, hidden) = refs[parts + 3 : 2 * parts + 3], refs[2 * parts + 3 :]
    start = 0
    for piece in rows:
        joined[start : start + piece.shape[0], :] = piece[...]
        start += piece.shape[0]
    width = 256
    for at in range(0, hidden.shape[1], width):
        columns = slice(at, at + width)
        gated = jnp.dot(joined[...], w_gate[:, columns], preferred_element_type=F32)
        lifted = jnp.dot(joined[...], w_up[:, columns], preferred_element_type=F32)
        hidden[:, columns] = (gated / (1.0 + jnp.exp(-gated)) * lifted).astype(BF16)
    for at in range(0, w_down.shape[1], width):
        columns = slice(at, at + width)
        made = jnp.dot(
            hidden[...], w_down[:, columns], preferred_element_type=F32
        ).astype(BF16)
        start = 0
        for out in outs:
            out[:, columns] = made[start : start + out.shape[0]]
            start += out.shape[0]


def add_kernel(pairs, *refs):
    lefts, rights, outs = refs[:pairs], refs[pairs : 2 * pairs], refs[2 * pairs :]
    share = len(outs) // pairs
    for i in range(pairs):
        start = 0
        for out in outs[i * share : (i + 1) * share]:
            at = slice(start, start + out.shape[0])
            out[...] = (lefts[i][at, :].astype(F32) + rights[i][at, :].astype(F32)).astype(BF16)
            start += out.shape[0]


def combine_kernel(count, *refs):
    route, blocks, out, joined = refs[0], refs[1 : 1 + count], refs[1 + count], refs[2 + count]
    start = 0
    for piece in blocks:
        joined[start : start + piece.shape[0], :] = piece[...]
        start += piece.shape[0]
    rows, lines = out.shape[0], joined.shape[0]
    place_of = lax.broadcasted_iota(jnp.int32, (rows, lines), 1).astype(F32)
    picked = [
        jnp.dot(
            (place_of == route[:, i : i + 1]).astype(F32).astype(BF16),
            joined[...],
            preferred_element_type=F32,
        )
        for i in range(2)
    ]
    gate = route[:, 2:3]
    out[...] = (gate * picked[0] + (1.0 - gate) * picked[1]).astype(BF16)


def add(lefts, rights, cuts):
    features = lefts[0].shape[1]
    outs = []
    for left in lefts:
        outs += [shape(left.shape[0] // cuts, features)] * cuts
    return call(
        functools.partial(add_kernel, len(lefts)),
        outs,
        [],
        sum(a.size for a in lefts),
        [*lefts, *rights],
        [VMEM] * (2 * len(lefts)),
    )


def gather(piece, small):
    if not small:
        return [lax.all_gather(piece, "exp", axis=0, tiled=True)]
    got = {0: piece}
    for bits in (6, 4, 2):
        got[bits] = swap(piece, "exp", bits)
    for bits in (0, 2, 4, 6):
        got[bits + 1] = swap(got[bits], "exp", 1)
    return [got[k] for k in range(8)]


def body(
    tokens, expert_ids, attn_gain, w_query, w_kv, w_out, moe_gain, router, w_gate, w_up, w_down
):
    features = tokens.shape[-1]
    inputs = tokens.reshape(-1, features)
    rows = inputs.shape[0]
    devices = lax.axis_size("exp")
    small = devices == 8
    ctx, position = lax.axis_index("ctx"), lax.axis_index("exp")
    core = ctx % 2
    me = position if small else jnp.zeros_like(position)
    place = jnp.stack([me, core, ctx]).astype(jnp.int32)
    heads = w_query.shape[1] // HD // lax.axis_size("ctx")

    attn_in = (rms_scaled(inputs.astype(F32)) * attn_gain).astype(BF16)
    piece = jnp.concatenate(
        [
            lax.dynamic_slice_in_dim(w_query, ctx * heads * HD, heads * HD, 1),
            lax.dynamic_slice_in_dim(w_kv, core * HD, HD, 1),
        ],
        axis=1,
    )
    weights = gather(piece, small)
    near = swap(attn_in, "ctx", 1)
    far = swap(attn_in, "ctx", 2)
    across = swap(far, "ctx", 1)
    half = w_out.shape[1] // 2
    out_piece = lax.dynamic_slice_in_dim(w_out, core * half, half, 1)
    out_own = gather(out_piece, small)
    out_theirs = [swap(w, "ctx", 1) for w in out_own]
    width = piece.shape[1]
    queries, mine = call(
        functools.partial(project_kernel, len(weights), heads),
        [shape(4 * rows, heads * HD), shape(4 * rows, HD)],
        [pltpu.VMEM((features, width), BF16), pltpu.VMEM((4 * rows, features), BF16)],
        8 * rows * features * width,
        [place, attn_in, near, far, across, *weights],
    )
    other = swap(mine, "ctx", 1)
    here, there = call(
        functools.partial(attend_kernel, heads),
        [shape(2 * rows, heads * HD)] * 2,
        [],
        16 * rows * rows * 4 * heads * HD,
        [place, queries, mine, other],
    )
    back = swap(there, "ctx", 2)

    def split(value):
        keep = lax.dynamic_slice_in_dim(value, core * rows, rows, 0)
        give = lax.dynamic_slice_in_dim(value, (1 - core) * rows, rows, 0)
        return keep, swap(give, "ctx", 1)

    context_0, context_1 = split(here)
    context_2, context_3 = split(back)

    experts = router.shape[1]
    capacity = max(2, 3 * rows * TOP // (2 * experts))
    lines = capacity * experts
    blocks = 8 if small else 1
    results = call(
        functools.partial(route_kernel, len(out_own), capacity, blocks),
        [shape(rows, features), shape(rows, 128, F32)]
        + [shape(lines // blocks, features)] * blocks,
        [
            pltpu.VMEM((2, w_out.shape[1], half), BF16),
            pltpu.VMEM((rows, w_out.shape[1]), BF16),
            pltpu.VMEM((rows, features), F32),
        ],
        2 * rows * features * (features + lines),
        [
            place,
            context_0,
            context_1,
            context_2,
            context_3,
            *out_own,
            *out_theirs,
            inputs,
            moe_gain.reshape(1, features),
            router,
            expert_ids.reshape(rows, TOP),
        ],
    )
    attention_out, route, buffers = results[0], results[1], results[2:]

    groups = ((0, 1, 2, 3), (4, 6), (5, 7)) if small else ((0,),)
    received = {}
    if small:
        received[0] = buffers[0]
        for k in (6, 4, 7, 5, 2, 3, 1):
            received[k] = swap(buffers[k], "exp", k)
    else:
        received[0] = lax.all_to_all(
            buffers[0], "exp", split_axis=0, concat_axis=0, tiled=True
        )
    returned = {}
    for group in groups:
        own = jnp.concatenate([received[k] for k in group]) if len(group) > 1 else received[group[0]]
        from_x = swap(own, "ctx", 2)
        from_core = swap(own, "ctx", 1)
        from_both = swap(from_x, "ctx", 1)
        taken = [own, from_x, from_core, from_both]
        count = own.shape[0]
        terms = call(
            functools.partial(expert_kernel, 4),
            [shape(count, features)] * 4,
            [
                pltpu.VMEM((4 * count, features), BF16),
                pltpu.VMEM((4 * count, w_gate.shape[-1]), BF16),
            ],
            24 * count * features * w_gate.shape[-1],
            [*taken, w_gate[0], w_up[0], w_down[0]],
            [VMEM] * 7,
        )
        core_x = swap(terms[3], "ctx", 1)
        core_own = swap(terms[2], "ctx", 1)
        (sum_x,) = add([terms[1]], [core_x], 1)
        x_own = swap(sum_x, "ctx", 2)
        (sum_own,) = add([terms[0]], [core_own], 1)
        for k, value in zip(group, add([sum_own], [x_own], len(group))):
            if small:
                returned[k] = swap(value, "exp", k) if k else value
            else:
                returned[k] = lax.all_to_all(
                    value, "exp", split_axis=0, concat_axis=0, tiled=True
                )
    (expert_mix,) = call(
        functools.partial(combine_kernel, blocks),
        [shape(rows, features)],
        [pltpu.VMEM((lines, features), BF16)],
        4 * rows * features * lines,
        [route, *[returned[k] for k in range(blocks)]],
        [VMEM] * (1 + blocks),
    )
    return (attention_out.reshape(tokens.shape), expert_mix.reshape(tokens.shape))


def solution(mesh):
    in_specs = (
        P("exp", "ctx", None),
        P("exp", "ctx", None),
        P(),
        P("exp", None),
        P("exp", None),
        P("exp", None),
        P(),
        P(),
        P("exp", None, "ctx"),
        P("exp", None, "ctx"),
        P("exp", "ctx", None),
    )
    out_specs = (P("exp", "ctx", None), P("exp", "ctx", None))
    return jax.shard_map(body, mesh=mesh, in_specs=in_specs, out_specs=out_specs, check_vma=False)
```

time: 277 us -> 146 us (0.53)
  waiting for transfers between devices: 135 us -> 63.7 us
  blocking collectives: 68.1 us -> 0 us
  starting transfers between devices: 5.85 us -> 53.8 us
  matrix products: 26 us -> 0 us
  Pallas kernels: 0 us -> 23.2 us
  local copies, waits for them, and re-layouts: 20.7 us -> 2.01 us
  between operations: 14 us -> 0.97 us
  other arithmetic: 6.86 us -> 2.33 us
    all_gather x3 -> x0, waiting for transfers between devices: 75.5 us -> none  [the longest x1 42.9 us: body(): lax.all_gather(w_out, 'exp', axis=0, tiled=True)]
    ppermute x0 -> x61, waiting for transfers between devices: none -> 63.7 us  [swap(): return lax.ppermute(value, axis, [(i, i ^ bits) for i in range(size)])]
    ppermute x0 -> x61, starting transfers between devices: none -> 53.8 us  [swap(): return lax.ppermute(value, axis, [(i, i ^ bits) for i in range(size)])]
    all_gather x3 -> x0, blocking collectives: 45.1 us -> none  [the longest x1 34.2 us: body(): lax.all_gather(w_kv, 'exp', axis=0, tiled=True)]
    reduce_scatter x1 -> x0, waiting for transfers between devices: 38.1 us -> none  [body(): lax.psum_scatter(jnp.einsum('ref,efd->red', hidden, w_down, preferred_ele...]
    dot_general x8 -> x0, matrix products: 26 us -> none  [the longest x1 11.7 us: body(): jnp.einsum('ref,efd->red', hidden, w_down, preferred_element_type=jnp.flo...]
    pallas_call x0 -> x16, Pallas kernels: none -> 23.2 us  [call(): pl.pallas_call(kernel, out_shape=outs, in_specs=[SMEM] + [VMEM] * (len(ar...]
    all_to_all x1 -> x0, blocking collectives: 23.1 us -> none  [body(): lax.all_to_all(buffer.reshape(capacity, experts, features), 'exp', split_...]
  transfers between devices with their start and end apart: 5 -> 61, of which waited for: 5 -> 23; matrix products, arithmetic and copies ran while one was open for 5% -> 1% of each run, Pallas kernels for 0% -> 14%
where the time goes in v1:
time: 146 us
  waiting for transfers between devices  63.7 us (44%)
  starting transfers between devices  53.8 us (37%)
  Pallas kernels  23.2 us (16%)
  other arithmetic  2.33 us (2%)
  local copies, waits for them, and re-layouts  2.01 us (1%)
    ppermute x61, waiting for transfers between devices, swap(): return lax.ppermute(value, axis, [(i, i ^ bits) for i in range(size)])  63.7 us
    ppermute x61, starting transfers between devices, swap(): return lax.ppermute(value, axis, [(i, i ^ bits) for i in range(size)])  53.8 us
    pallas_call x16, Pallas kernels, call(): pl.pallas_call(kernel, out_shape=outs, in_specs=[SMEM] + [VMEM] * (len(ar...  23.2 us
  transfers between devices with their start and end apart: 61, of which 23 were waited for; matrix products, arithmetic and copies ran while one was open for 1% of the time, Pallas kernels for 14%

profile of v1, /device:TPU:0, one launch (start us, length us, event | category | flops | bytes accessed | tf_op | source)
XLA Modules:
  0.0 146.0 jit_solution(17164257300833335406)
XLA Ops:
  2.9 3.0 %collective-permute-start.1 = (bf16[128,1024]{1,0:T(8,128)(2,1)S(1)}, bf16[128,1024]{1,0:T(8,128)(2,1)S(1)}, u32[]{:S(2)}, u32[]{:S(2)}) collective-permute-start(bf16[128,1024]{1,0:T(8,128)(2,1)S(1)} %fusion.2.refs_0_), channel_id=1, source_target_pairs={{0,16},{8,24},{16,0},{24,8},{1,17},{9,25},{17,1},{25,9},{2,18},{10... | collective-permute-start | bytes 786440 | tf_op jit(solution)/shard_map/ppermute | solution.py:25
  9.2 2.6 %collective-permute-start.6 = (bf16[128,384]{1,0:T(8,128)(2,1)S(1)}, bf16[128,384]{1,0:T(8,128)(2,1)S(1)}, u32[]{:S(2)}, u32[]{:S(2)}) collective-permute-start(bf16[128,384]{1,0:T(8,128)(2,1)S(1)} %pad_maximum_fusion.refs_4_), channel_id=1, source_target_pairs={{0,4},{1,5},{2,6},{3,7},{4,0},{5,1},{6,2},{7,3},{8,12},{9,13},{10,... | collective-permute-start | bytes 294920 | tf_op jit(solution)/shard_map/ppermute | solution.py:25
  13.8 5.9 %collective-permute-done.6.refs_8_ = bf16[128,384]{1,0:T(8,128)(2,1)S(1)} collective-permute-done((bf16[128,384]{1,0:T(8,128)(2,1)S(1)}, bf16[128,384]{1,0:T(8,128)(2,1)S(1)}, u32[]{:S(2)}, u32[]{:S(2)}) %collective-permute-start.6) | collective-permute-done | bytes 98336 | tf_op jit(solution)/shard_map/ppermute | solution.py:25
  23.2 2.1 %collective-permute-done.5.refs_7_ = bf16[128,384]{1,0:T(8,128)(2,1)S(1)} collective-permute-done((bf16[128,384]{1,0:T(8,128)(2,1)S(1)}, bf16[128,384]{1,0:T(8,128)(2,1)S(1)}, u32[]{:S(2)}, u32[]{:S(2)}) %collective-permute-start.5) | collective-permute-done | bytes 98336 | tf_op jit(solution)/shard_map/ppermute | solution.py:25
  25.3 2.0 %collective-permute-done.7.refs_9_ = bf16[128,384]{1,0:T(8,128)(2,1)S(1)} collective-permute-done((bf16[128,384]{1,0:T(8,128)(2,1)S(1)}, bf16[128,384]{1,0:T(8,128)(2,1)S(1)}, u32[]{:S(2)}, u32[]{:S(2)}) %collective-permute-start.7) | collective-permute-done | bytes 98336 | tf_op jit(solution)/shard_map/ppermute | solution.py:25
  28.9 1.9 %collective-permute-start.19 = (bf16[128,512]{1,0:T(8,128)(2,1)S(1)}, bf16[128,512]{1,0:T(8,128)(2,1)S(1)}, u32[]{:S(2)}, u32[]{:S(2)}) collective-permute-start(bf16[128,512]{1,0:T(8,128)(2,1)S(1)} %constant_dynamic-slice_fusion.refs_4_), channel_id=1, source_target_pairs={{0,6},{1,7},{2,4},{3,5},{4,2},{5,3},{6,0},{7,1},{8,14},{9,15},{10,... | collective-permute-start | bytes 393224 | tf_op jit(solution)/shard_map/ppermute | solution.py:25
  34.3 3.9 %collective-permute-done.17.refs_8_ = bf16[128,512]{1,0:T(8,128)(2,1)S(1)} collective-permute-done((bf16[128,512]{1,0:T(8,128)(2,1)S(1)}, bf16[128,512]{1,0:T(8,128)(2,1)S(1)}, u32[]{:S(2)}, u32[]{:S(2)}) %collective-permute-start.17) | collective-permute-done | bytes 131104 | tf_op jit(solution)/shard_map/ppermute | solution.py:25
  46.8 2.7 %collective-permute-done.12 = bf16[256,256]{1,0:T(8,128)(2,1)S(1)} collective-permute-done((bf16[256,256]{1,0:T(8,128)(2,1)S(1)}, bf16[256,256]{1,0:T(8,128)(2,1)S(1)}, u32[]{:S(2)}, u32[]{:S(2)}) %collective-permute-start.12) | collective-permute-done | bytes 131104 | tf_op jit(solution)/shard_map/ppermute | solution.py:25
  51.4 2.2 %shard_map.124 = (bf16[128,1024]{1,0:T(8,128)(2,1)}, f32[128,128]{1,0:T(8,128)S(1)}, bf16[48,1024]{1,0:T(8,128)(2,1)S(1)}, bf16[48,1024]{1,0:T(8,128)(2,1)S(1)},...) custom-call(s32[3]{0:T(128)S(1)} %pad_add_fusion.place, ...), custom_call_target="tpu_custom_call" | custom-call | flops 369098752 | bytes 3757068 | tf_op jit(solution)/shard_map/pallas_call | solution.py:32
  59.9 2.0 %collective-permute-done.31 = bf16[48,1024]{1,0:T(8,128)(2,1)S(1)} collective-permute-done((bf16[48,1024]{1,0:T(8,128)(2,1)S(1)}, bf16[48,1024]{1,0:T(8,128)(2,1)S(1)}, u32[]{:S(2)}, u32[]{:S(2)}) %collective-permute-start.31) | collective-permute-done | bytes 98336 | tf_op jit(solution)/shard_map/ppermute | solution.py:25
  62.4 2.0 %collective-permute-start.50 = (bf16[48,1024]{1,0:T(8,128)(2,1)S(1)}, bf16[48,1024]{1,0:T(8,128)(2,1)S(1)}, u32[]{:S(2)}, u32[]{:S(2)}) collective-permute-start(bf16[48,1024]{1,0:T(8,128)(2,1)S(1)} %get-tuple-element.61), channel_id=1, source_target_pairs={{0,5},{1,4},{2,7},{3,6},{4,1},{5,0},{6,3},{7,2},{8,13},{9,12},{10,... | collective-permute-start | bytes 294920 | tf_op jit(solution)/shard_map/ppermute | solution.py:25
  67.5 1.7 %collective-permute-start.42 = (bf16[48,1024]{1,0:T(8,128)(2,1)S(1)}, bf16[48,1024]{1,0:T(8,128)(2,1)S(1)}, u32[]{:S(2)}, u32[]{:S(2)}) collective-permute-start(bf16[48,1024]{1,0:T(8,128)(2,1)S(1)} %get-tuple-element.55), channel_id=1, source_target_pairs={{0,6},{1,7},{2,4},{3,5},{4,2},{5,3},{6,0},{7,1},{8,14},{9,15},{10,... | collective-permute-start | bytes 294920 | tf_op jit(solution)/shard_map/ppermute | solution.py:25
  69.2 8.1 %collective-permute-done.50 = bf16[48,1024]{1,0:T(8,128)(2,1)S(1)} collective-permute-done((bf16[48,1024]{1,0:T(8,128)(2,1)S(1)}, bf16[48,1024]{1,0:T(8,128)(2,1)S(1)}, u32[]{:S(2)}, u32[]{:S(2)}) %collective-permute-start.50) | collective-permute-done | bytes 98336 | tf_op jit(solution)/shard_map/ppermute | solution.py:25
  82.0 3.1 %collective-permute-done.52.refs_1_ = bf16[96,1024]{1,0:T(8,128)(2,1)S(1)} collective-permute-done((bf16[96,1024]{1,0:T(8,128)(2,1)S(1)}, bf16[96,1024]{1,0:T(8,128)(2,1)S(1)}, u32[]{:S(2)}, u32[]{:S(2)}) %collective-permute-start.52) | collective-permute-done | bytes 196640 | tf_op jit(solution)/shard_map/ppermute | solution.py:25
  85.1 3.8 %collective-permute-done.43.refs_1_ = bf16[96,1024]{1,0:T(8,128)(2,1)S(1)} collective-permute-done((bf16[96,1024]{1,0:T(8,128)(2,1)S(1)}, bf16[96,1024]{1,0:T(8,128)(2,1)S(1)}, u32[]{:S(2)}, u32[]{:S(2)}) %collective-permute-start.43) | collective-permute-done | bytes 196640 | tf_op jit(solution)/shard_map/ppermute | solution.py:25
  89.5 7.4 %shard_map.125 = (bf16[192,1024]{1,0:T(8,128)(2,1)S(1)}, bf16[192,1024]{1,0:T(8,128)(2,1)S(1)}, bf16[192,1024]{1,0:T(8,128)(2,1)S(1)}, bf16[192,1024]{1,0:T(8,128)(2,1)S(1)}) custom-call(bf16[192,1024]{1,0:T(8,128)(2,1)S(1)} %constant_dynamic-update-slice_fusion.refs_0_, bf16[192,1024]{1,0:T(8,128)(2,1)S(1)} %collective-permute-done.32.refs_1_, ...), custom_call_target="tpu_custom_call" | custom-call | flops 4831838208 | bytes 9437184 | tf_op jit(solution)/shard_map/pallas_call | solution.py:32
  97.0 4.4 %shard_map.133 = (bf16[96,1024]{1,0:T(8,128)(2,1)S(1)}, bf16[96,1024]{1,0:T(8,128)(2,1)S(1)}, bf16[96,1024]{1,0:T(8,128)(2,1)S(1)}, bf16[96,1024]{1,0:T(8,128)(2,1)S(1)}) custom-call(bf16[96,1024]{1,0:T(8,128)(2,1)S(1)} %constant_dynamic-update-slice_fusion.6.refs_0_, bf16[96,1024]{1,0:T(8,128)(2,1)S(1)} %collective-permute-done.52.refs_1_, ...), custom_call_target="tpu_custom_call" | custom-call | flops 2415919104 | bytes 7864320 | tf_op jit(solution)/shard_map/pallas_call | solution.py:32
  102.0 4.2 %shard_map.129 = (bf16[96,1024]{1,0:T(8,128)(2,1)S(1)}, bf16[96,1024]{1,0:T(8,128)(2,1)S(1)}, bf16[96,1024]{1,0:T(8,128)(2,1)S(1)}, bf16[96,1024]{1,0:T(8,128)(2,1)S(1)}) custom-call(bf16[96,1024]{1,0:T(8,128)(2,1)S(1)} %constant_dynamic-update-slice_fusion.4.refs_0_, bf16[96,1024]{1,0:T(8,128)(2,1)S(1)} %collective-permute-done.43.refs_1_, ...), custom_call_target="tpu_custom_call" | custom-call | flops 2415919104 | bytes 7864320 | tf_op jit(solution)/shard_map/pallas_call | solution.py:32
  110.9 12.3 %collective-permute-done.57.refs_1_ = bf16[96,1024]{1,0:T(8,128)(2,1)S(1)} collective-permute-done((bf16[96,1024]{1,0:T(8,128)(2,1)S(1)}, bf16[96,1024]{1,0:T(8,128)(2,1)S(1)}, u32[]{:S(2)}, u32[]{:S(2)}) %collective-permute-start.57) | collective-permute-done | bytes 196640 | tf_op jit(solution)/shard_map/ppermute | solution.py:25
  123.2 1.9 %collective-permute-start.58 = (bf16[48,1024]{1,0:T(8,128)(2,1)S(1)}, bf16[48,1024]{1,0:T(8,128)(2,1)S(1)}, u32[]{:S(2)}, u32[]{:S(2)}) collective-permute-start(bf16[48,1024]{1,0:T(8,128)(2,1)S(1)} %get-tuple-element.67), channel_id=1, source_target_pairs={{0,5},{1,4},{2,7},{3,6},{4,1},{5,0},{6,3},{7,2},{8,13},{9,12},{10,... | collective-permute-start | bytes 294920 | tf_op jit(solution)/shard_map/ppermute | solution.py:25
  125.1 2.4 %collective-permute-start.60 = (bf16[48,1024]{1,0:T(8,128)(2,1)S(1)}, bf16[48,1024]{1,0:T(8,128)(2,1)S(1)}, u32[]{:S(2)}, u32[]{:S(2)}) collective-permute-start(bf16[48,1024]{1,0:T(8,128)(2,1)S(1)} %get-tuple-element.69), channel_id=1, source_target_pairs={{0,7},{1,6},{2,5},{3,4},{4,3},{5,2},{6,1},{7,0},{8,15},{9,14},{10,... | collective-permute-start | bytes 294920 | tf_op jit(solution)/shard_map/ppermute | solution.py:25
  131.2 7.0 %collective-permute-done.58.refs_6_ = bf16[48,1024]{1,0:T(8,128)(2,1)S(1)} collective-permute-done((bf16[48,1024]{1,0:T(8,128)(2,1)S(1)}, bf16[48,1024]{1,0:T(8,128)(2,1)S(1)}, u32[]{:S(2)}, u32[]{:S(2)}) %collective-permute-start.58) | collective-permute-done | bytes 98336 | tf_op jit(solution)/shard_map/ppermute | solution.py:25
  138.2 2.6 %collective-permute-start.40 = (bf16[48,1024]{1,0:T(8,128)(2,1)S(1)}, bf16[48,1024]{1,0:T(8,128)(2,1)S(1)}, u32[]{:S(2)}, u32[]{:S(2)}) collective-permute-start(bf16[48,1024]{1,0:T(8,128)(2,1)S(1)} %get-tuple-element.53), channel_id=1, source_target_pairs={{0,3},{1,2},{2,1},{3,0},{4,7},{5,6},{6,5},{7,4},{8,11},{9,10},{10,... | collective-permute-start | bytes 294920 | tf_op jit(solution)/shard_map/ppermute | solution.py:25
  141.4 2.4 %collective-permute-done.39.refs_3_ = bf16[48,1024]{1,0:T(8,128)(2,1)S(1)} collective-permute-done((bf16[48,1024]{1,0:T(8,128)(2,1)S(1)}, bf16[48,1024]{1,0:T(8,128)(2,1)S(1)}, u32[]{:S(2)}, u32[]{:S(2)}) %collective-permute-start.39) | collective-permute-done | bytes 98336 | tf_op jit(solution)/shard_map/ppermute | solution.py:25
  (148 shorter events, 53.1 us)
Async XLA Ops:
  2.9 10.9 %collective-permute-start.1 = (bf16[128,1024]{1,0:T(8,128)(2,1)S(1)}, bf16[128,1024]{1,0:T(8,128)(2,1)S(1)}, u32[]{:S(2)}, u32[]{:S(2)}) collective-permute-start(bf16[128,1024]{1,0:T(8,128)(2,1)S(1)} %fusion.2.refs_0_), channel_id=1, source_target_pairs={{0,16},{8,24},{16,0},{24,8},{1,17},{9,25},{17,1},{25,9},{2,18},{10... | collective-permute-start | bytes 786440 | tf_op jit(solution)/shard_map/ppermute | solution.py:25
  9.2 21.7 %collective-permute-start = (bf16[128,1024]{1,0:T(8,128)(2,1)S(1)}, bf16[128,1024]{1,0:T(8,128)(2,1)S(1)}, u32[]{:S(2)}, u32[]{:S(2)}) collective-permute-start(bf16[128,1024]{1,0:T(8,128)(2,1)S(1)} %fusion.2.refs_0_), channel_id=1, source_target_pairs={{0,8},{8,0},{16,24},{24,16},{1,9},{9,1},{17,25},{25,17},{2,10},{10... | collective-permute-start | bytes 786440 | tf_op jit(solution)/shard_map/ppermute | solution.py:25
  13.8 18.5 %collective-permute-start.2 = (bf16[128,1024]{1,0:T(8,128)(2,1)S(1)}, bf16[128,1024]{1,0:T(8,128)(2,1)S(1)}, u32[]{:S(2)}, u32[]{:S(2)}) collective-permute-start(bf16[128,1024]{1,0:T(8,128)(2,1)S(1)} %collective-permute-done.1.refs_2_), channel_id=1, source_target_pairs={{0,8},{8,0},{16,24},{24,16},{1,9},{9,1},{17,25},{25,17},{2,10},{10... | collective-permute-start | bytes 786440 | tf_op jit(solution)/shard_map/ppermute | solution.py:25
  27.3 10.9 %collective-permute-start.17 = (bf16[128,512]{1,0:T(8,128)(2,1)S(1)}, bf16[128,512]{1,0:T(8,128)(2,1)S(1)}, u32[]{:S(2)}, u32[]{:S(2)}) collective-permute-start(bf16[128,512]{1,0:T(8,128)(2,1)S(1)} %constant_dynamic-slice_fusion.refs_4_), channel_id=1, source_target_pairs={{0,4},{1,5},{2,6},{3,7},{4,0},{5,1},{6,2},{7,3},{8,12},{9,13},{10,... | collective-permute-start | bytes 393224 | tf_op jit(solution)/shard_map/ppermute | solution.py:25
  28.9 10.8 %collective-permute-start.19 = (bf16[128,512]{1,0:T(8,128)(2,1)S(1)}, bf16[128,512]{1,0:T(8,128)(2,1)S(1)}, u32[]{:S(2)}, u32[]{:S(2)}) collective-permute-start(bf16[128,512]{1,0:T(8,128)(2,1)S(1)} %constant_dynamic-slice_fusion.refs_4_), channel_id=1, source_target_pairs={{0,6},{1,7},{2,4},{3,5},{4,2},{5,3},{6,0},{7,1},{8,14},{9,15},{10,... | collective-permute-start | bytes 393224 | tf_op jit(solution)/shard_map/ppermute | solution.py:25
  61.8 17.1 %collective-permute-start.32 = (bf16[192,1024]{1,0:T(8,128)(2,1)S(1)}, bf16[192,1024]{1,0:T(8,128)(2,1)S(1)}, u32[]{:S(2)}, u32[]{:S(2)}) collective-permute-start(bf16[192,1024]{1,0:T(8,128)(2,1)S(1)} %constant_dynamic-update-slice_fusion.refs_0_), channel_id=1, source_target_pairs={{0,16},{8,24},{16,0},{24,8},{1,17},{9,25},{17,1},{25,9},{2,18},{10... | collective-permute-start | bytes 1179656 | tf_op jit(solution)/shard_map/ppermute | solution.py:25
  62.4 14.9 %collective-permute-start.50 = (bf16[48,1024]{1,0:T(8,128)(2,1)S(1)}, bf16[48,1024]{1,0:T(8,128)(2,1)S(1)}, u32[]{:S(2)}, u32[]{:S(2)}) collective-permute-start(bf16[48,1024]{1,0:T(8,128)(2,1)S(1)} %get-tuple-element.61), channel_id=1, source_target_pairs={{0,5},{1,4},{2,7},{3,6},{4,1},{5,0},{6,3},{7,2},{8,13},{9,12},{10,... | collective-permute-start | bytes 294920 | tf_op jit(solution)/shard_map/ppermute | solution.py:25
  64.5 12.9 %collective-permute-start.51 = (bf16[48,1024]{1,0:T(8,128)(2,1)S(1)}, bf16[48,1024]{1,0:T(8,128)(2,1)S(1)}, u32[]{:S(2)}, u32[]{:S(2)}) collective-permute-start(bf16[48,1024]{1,0:T(8,128)(2,1)S(1)} %get-tuple-element.62), channel_id=1, source_target_pairs={{0,7},{1,6},{2,5},{3,4},{4,3},{5,2},{6,1},{7,0},{8,15},{9,14},{10,... | collective-permute-start | bytes 294920 | tf_op jit(solution)/shard_map/ppermute | solution.py:25
  66.2 14.2 %collective-permute-start.41 = (bf16[48,1024]{1,0:T(8,128)(2,1)S(1)}, bf16[48,1024]{1,0:T(8,128)(2,1)S(1)}, u32[]{:S(2)}, u32[]{:S(2)}) collective-permute-start(bf16[48,1024]{1,0:T(8,128)(2,1)S(1)} %get-tuple-element.54), channel_id=1, source_target_pairs={{0,4},{1,5},{2,6},{3,7},{4,0},{5,1},{6,2},{7,3},{8,12},{9,13},{10,... | collective-permute-start | bytes 294920 | tf_op jit(solution)/shard_map/ppermute | solution.py:25
  67.5 13.0 %collective-permute-start.42 = (bf16[48,1024]{1,0:T(8,128)(2,1)S(1)}, bf16[48,1024]{1,0:T(8,128)(2,1)S(1)}, u32[]{:S(2)}, u32[]{:S(2)}) collective-permute-start(bf16[48,1024]{1,0:T(8,128)(2,1)S(1)} %get-tuple-element.55), channel_id=1, source_target_pairs={{0,6},{1,7},{2,4},{3,5},{4,2},{5,3},{6,0},{7,1},{8,14},{9,15},{10,... | collective-permute-start | bytes 294920 | tf_op jit(solution)/shard_map/ppermute | solution.py:25
  77.3 11.6 %collective-permute-start.33 = (bf16[192,1024]{1,0:T(8,128)(2,1)S(1)}, bf16[192,1024]{1,0:T(8,128)(2,1)S(1)}, u32[]{:S(2)}, u32[]{:S(2)}) collective-permute-start(bf16[192,1024]{1,0:T(8,128)(2,1)S(1)} %constant_dynamic-update-slice_fusion.refs_0_), channel_id=1, source_target_pairs={{0,8},{8,0},{16,24},{24,16},{1,9},{9,1},{17,25},{25,17},{2,10},{10... | collective-permute-start | bytes 1179656 | tf_op jit(solution)/shard_map/ppermute | solution.py:25
  82.0 15.0 %collective-permute-start.53 = (bf16[96,1024]{1,0:T(8,128)(2,1)S(1)}, bf16[96,1024]{1,0:T(8,128)(2,1)S(1)}, u32[]{:S(2)}, u32[]{:S(2)}) collective-permute-start(bf16[96,1024]{1,0:T(8,128)(2,1)S(1)} %constant_dynamic-update-slice_fusion.6.refs_0_), channel_id=1, source_target_pairs={{0,8},{8,0},{16,24},{24,16},{1,9},{9,1},{17,25},{25,17},{2,10},{10... | collective-permute-start | bytes 589832 | tf_op jit(solution)/shard_map/ppermute | solution.py:25
  85.1 16.9 %collective-permute-start.44 = (bf16[96,1024]{1,0:T(8,128)(2,1)S(1)}, bf16[96,1024]{1,0:T(8,128)(2,1)S(1)}, u32[]{:S(2)}, u32[]{:S(2)}) collective-permute-start(bf16[96,1024]{1,0:T(8,128)(2,1)S(1)} %constant_dynamic-update-slice_fusion.4.refs_0_), channel_id=1, source_target_pairs={{0,8},{8,0},{16,24},{24,16},{1,9},{9,1},{17,25},{25,17},{2,10},{10... | collective-permute-start | bytes 589832 | tf_op jit(solution)/shard_map/ppermute | solution.py:25
  89.0 13.0 %collective-permute-start.45 = (bf16[96,1024]{1,0:T(8,128)(2,1)S(1)}, bf16[96,1024]{1,0:T(8,128)(2,1)S(1)}, u32[]{:S(2)}, u32[]{:S(2)}) collective-permute-start(bf16[96,1024]{1,0:T(8,128)(2,1)S(1)} %collective-permute-done.43.refs_1_), channel_id=1, source_target_pairs={{0,8},{8,0},{16,24},{24,16},{1,9},{9,1},{17,25},{25,17},{2,10},{10... | collective-permute-start | bytes 589832 | tf_op jit(solution)/shard_map/ppermute | solution.py:25
  106.8 21.9 %collective-permute-start.35 = (bf16[192,1024]{1,0:T(8,128)(2,1)S(1)}, bf16[192,1024]{1,0:T(8,128)(2,1)S(1)}, u32[]{:S(2)}, u32[]{:S(2)}) collective-permute-start(bf16[192,1024]{1,0:T(8,128)(2,1)S(1)} %get-tuple-element.47), channel_id=1, source_target_pairs={{0,8},{8,0},{16,24},{24,16},{1,9},{9,1},{17,25},{25,17},{2,10},{10... | collective-permute-start | bytes 1179656 | tf_op jit(solution)/shard_map/ppermute | solution.py:25
  107.0 23.5 %collective-permute-start.37 = (bf16[192,1024]{1,0:T(8,128)(2,1)S(1)}, bf16[192,1024]{1,0:T(8,128)(2,1)S(1)}, u32[]{:S(2)}, u32[]{:S(2)}) collective-permute-start(bf16[192,1024]{1,0:T(8,128)(2,1)S(1)} %shard_map.127), channel_id=1, source_target_pairs={{0,16},{8,24},{16,0},{24,8},{1,17},{9,25},{17,1},{25,9},{2,18},{10... | collective-permute-start | bytes 1179656 | tf_op jit(solution)/shard_map/ppermute | solution.py:25
  108.6 14.6 %collective-permute-start.57 = (bf16[96,1024]{1,0:T(8,128)(2,1)S(1)}, bf16[96,1024]{1,0:T(8,128)(2,1)S(1)}, u32[]{:S(2)}, u32[]{:S(2)}) collective-permute-start(bf16[96,1024]{1,0:T(8,128)(2,1)S(1)} %shard_map.135), channel_id=1, source_target_pairs={{0,16},{8,24},{16,0},{24,8},{1,17},{9,25},{17,1},{25,9},{2,18},{10... | collective-permute-start | bytes 589832 | tf_op jit(solution)/shard_map/ppermute | solution.py:25
  109.2 15.9 %collective-permute-start.46 = (bf16[96,1024]{1,0:T(8,128)(2,1)S(1)}, bf16[96,1024]{1,0:T(8,128)(2,1)S(1)}, u32[]{:S(2)}, u32[]{:S(2)}) collective-permute-start(bf16[96,1024]{1,0:T(8,128)(2,1)S(1)} %get-tuple-element.57), channel_id=1, source_target_pairs={{0,8},{8,0},{16,24},{24,16},{1,9},{9,1},{17,25},{25,17},{2,10},{10... | collective-permute-start | bytes 589832 | tf_op jit(solution)/shard_map/ppermute | solution.py:25
  109.3 18.4 %collective-permute-start.48 = (bf16[96,1024]{1,0:T(8,128)(2,1)S(1)}, bf16[96,1024]{1,0:T(8,128)(2,1)S(1)}, u32[]{:S(2)}, u32[]{:S(2)}) collective-permute-start(bf16[96,1024]{1,0:T(8,128)(2,1)S(1)} %shard_map.131), channel_id=1, source_target_pairs={{0,16},{8,24},{16,0},{24,8},{1,17},{9,25},{17,1},{25,9},{2,18},{10... | collective-permute-start | bytes 589832 | tf_op jit(solution)/shard_map/ppermute | solution.py:25
  123.2 15.0 %collective-permute-start.58 = (bf16[48,1024]{1,0:T(8,128)(2,1)S(1)}, bf16[48,1024]{1,0:T(8,128)(2,1)S(1)}, u32[]{:S(2)}, u32[]{:S(2)}) collective-permute-start(bf16[48,1024]{1,0:T(8,128)(2,1)S(1)} %get-tuple-element.67), channel_id=1, source_target_pairs={{0,5},{1,4},{2,7},{3,6},{4,1},{5,0},{6,3},{7,2},{8,13},{9,12},{10,... | collective-permute-start | bytes 294920 | tf_op jit(solution)/shard_map/ppermute | solution.py:25
  125.1 13.1 %collective-permute-start.60 = (bf16[48,1024]{1,0:T(8,128)(2,1)S(1)}, bf16[48,1024]{1,0:T(8,128)(2,1)S(1)}, u32[]{:S(2)}, u32[]{:S(2)}) collective-permute-start(bf16[48,1024]{1,0:T(8,128)(2,1)S(1)} %get-tuple-element.69), channel_id=1, source_target_pairs={{0,7},{1,6},{2,5},{3,4},{4,3},{5,2},{6,1},{7,0},{8,15},{9,14},{10,... | collective-permute-start | bytes 294920 | tf_op jit(solution)/shard_map/ppermute | solution.py:25
  127.7 13.7 %collective-permute-start.49 = (bf16[48,1024]{1,0:T(8,128)(2,1)S(1)}, bf16[48,1024]{1,0:T(8,128)(2,1)S(1)}, u32[]{:S(2)}, u32[]{:S(2)}) collective-permute-start(bf16[48,1024]{1,0:T(8,128)(2,1)S(1)} %get-tuple-element.60), channel_id=1, source_target_pairs={{0,4},{1,5},{2,6},{3,7},{4,0},{5,1},{6,2},{7,3},{8,12},{9,13},{10,... | collective-permute-start | bytes 294920 | tf_op jit(solution)/shard_map/ppermute | solution.py:25
  128.7 12.7 %collective-permute-start.59 = (bf16[48,1024]{1,0:T(8,128)(2,1)S(1)}, bf16[48,1024]{1,0:T(8,128)(2,1)S(1)}, u32[]{:S(2)}, u32[]{:S(2)}) collective-permute-start(bf16[48,1024]{1,0:T(8,128)(2,1)S(1)} %get-tuple-element.68), channel_id=1, source_target_pairs={{0,6},{1,7},{2,4},{3,5},{4,2},{5,3},{6,0},{7,1},{8,14},{9,15},{10,... | collective-permute-start | bytes 294920 | tf_op jit(solution)/shard_map/ppermute | solution.py:25
  130.7 10.8 %collective-permute-start.38 = (bf16[48,1024]{1,0:T(8,128)(2,1)S(1)}, bf16[48,1024]{1,0:T(8,128)(2,1)S(1)}, u32[]{:S(2)}, u32[]{:S(2)}) collective-permute-start(bf16[48,1024]{1,0:T(8,128)(2,1)S(1)} %get-tuple-element.51), channel_id=1, source_target_pairs={{0,1},{1,0},{2,3},{3,2},{4,5},{5,4},{6,7},{7,6},{8,9},{9,8},{10,11... | collective-permute-start | bytes 294920 | tf_op jit(solution)/shard_map/ppermute | solution.py:25
  (44 other events, 472.1 us)

commit v2 on v1

--- a/solution.py
+++ b/solution.py
@@ -35,7 +35,7 @@
         in_specs=[SMEM] + [VMEM] * (len(args) - 1) if specs is None else specs,
         out_specs=[VMEM] * len(outs),
         scratch_shapes=scratch,
-        cost_estimate=pl.CostEstimate(flops=flops, bytes_accessed=moved, transcendentals=0),
+        cost_estimate=pl.CostEstimate(flops=flops * 1, bytes_accessed=moved * 1, transcendentals=0),
         compiler_params=pltpu.CompilerParams(vmem_limit_bytes=48 * 1024 * 1024),
     )(*args)
 
@@ -224,6 +224,10 @@
     )
 
 
+def after(value, earlier):
+    return lax.optimization_barrier((value, earlier))[0]
+
+
 def gather(piece, small):
     if not small:
         return [lax.all_gather(piece, "exp", axis=0, tiled=True)]
@@ -321,23 +325,33 @@
     )
     attention_out, route, buffers = results[0], results[1], results[2:]
 
-    groups = ((0, 1, 2, 3), (4, 6), (5, 7)) if small else ((0,),)
+    groups = ((4, 5), (6, 7), (0, 1, 2, 3)) if small else ((0,),)
     received = {}
     if small:
         received[0] = buffers[0]
-        for k in (6, 4, 7, 5, 2, 3, 1):
+        for k in (5, 4, 7, 6, 3, 2, 1):
             received[k] = swap(buffers[k], "exp", k)
     else:
         received[0] = lax.all_to_all(
             buffers[0], "exp", split_axis=0, concat_axis=0, tiled=True
         )
+    owns, earlier = [], None
+    for group in groups:
+        blocks_in = [received[k] for k in group]
+        if earlier is not None:
+            blocks_in = [after(b, earlier) for b in blocks_in]
+        own = jnp.concatenate(blocks_in) if len(group) > 1 else blocks_in[0]
+        owns.append(own)
+        earlier = own
     returned = {}
-    for group in groups:
-        own = jnp.concatenate([received[k] for k in group]) if len(group) > 1 else received[group[0]]
+    earlier, waiting = None, None
+    for group, own in zip(groups, owns):
         from_x = swap(own, "ctx", 2)
         from_core = swap(own, "ctx", 1)
         from_both = swap(from_x, "ctx", 1)
         taken = [own, from_x, from_core, from_both]
+        if earlier is not None:
+            taken = list(lax.optimization_barrier((*taken, *earlier))[:4])
         count = own.shape[0]
         terms = call(
             functools.partial(expert_kernel, 4),
@@ -355,7 +369,10 @@
         (sum_x,) = add([terms[1]], [core_x], 1)
         x_own = swap(sum_x, "ctx", 2)
         (sum_own,) = add([terms[0]], [core_own], 1)
-        for k, value in zip(group, add([sum_own], [x_own], len(group))):
+        final = add([sum_own], [x_own], len(group))
+        earlier = [sum_x, sum_own] + (waiting or [])
+        waiting = list(final)
+        for k, value in zip(group, final):
             if small:
                 returned[k] = swap(value, "exp", k) if k else value
             else:

time: 146 us -> 138 us (0.945)
  waiting for transfers between devices: 63.7 us -> 57.8 us
  starting transfers between devices: 53.8 us -> 52 us
    ppermute x61, waiting for transfers between devices: 63.7 us -> 57.8 us  [swap(): return lax.ppermute(value, axis, [(i, i ^ bits) for i in range(size)])]
    ppermute x61, starting transfers between devices: 53.8 us -> 52 us  [swap(): return lax.ppermute(value, axis, [(i, i ^ bits) for i in range(size)])]
  transfers between devices with their start and end apart: 61 -> 61, of which waited for: 23 -> 24; matrix products, arithmetic and copies ran while one was open for 1% -> 1% of each run, Pallas kernels for 14% -> 9%
where the time goes in v2:
time: 138 us
  waiting for transfers between devices  57.8 us (42%)
  starting transfers between devices  52 us (38%)
  Pallas kernels  23 us (17%)
  other arithmetic  2.33 us (2%)
  local copies, waits for them, and re-layouts  2.01 us (1%)
    ppermute x61, waiting for transfers between devices, swap(): return lax.ppermute(value, axis, [(i, i ^ bits) for i in range(size)])  57.8 us
    ppermute x61, starting transfers between devices, swap(): return lax.ppermute(value, axis, [(i, i ^ bits) for i in range(size)])  52 us
    pallas_call x16, Pallas kernels, call(): pl.pallas_call(kernel, out_shape=outs, in_specs=[SMEM] + [VMEM] * (len(ar...  23 us
  transfers between devices with their start and end apart: 61, of which 24 were waited for; matrix products, arithmetic and copies ran while one was open for 1% of the time, Pallas kernels for 9%

profile of v2, /device:TPU:0, one launch (start us, length us, event | category | flops | bytes accessed | tf_op | source)
XLA Modules:
  0.0 138.1 jit_solution(1944964401382131723)
XLA Ops:
  2.9 3.0 %collective-permute-start.1 = (bf16[128,1024]{1,0:T(8,128)(2,1)S(1)}, bf16[128,1024]{1,0:T(8,128)(2,1)S(1)}, u32[]{:S(2)}, u32[]{:S(2)}) collective-permute-start(bf16[128,1024]{1,0:T(8,128)(2,1)S(1)} %fusion.2.refs_0_), channel_id=1, source_target_pairs={{0,16},{8,24},{16,0},{24,8},{1,17},{9,25},{17,1},{25,9},{2,18},{10... | collective-permute-start | bytes 786440 | tf_op jit(solution)/shard_map/ppermute | solution.py:25
  9.2 2.6 %collective-permute-start.6 = (bf16[128,384]{1,0:T(8,128)(2,1)S(1)}, bf16[128,384]{1,0:T(8,128)(2,1)S(1)}, u32[]{:S(2)}, u32[]{:S(2)}) collective-permute-start(bf16[128,384]{1,0:T(8,128)(2,1)S(1)} %pad_maximum_fusion.refs_4_), channel_id=1, source_target_pairs={{0,4},{1,5},{2,6},{3,7},{4,0},{5,1},{6,2},{7,3},{8,12},{9,13},{10,... | collective-permute-start | bytes 294920 | tf_op jit(solution)/shard_map/ppermute | solution.py:25
  13.8 5.9 %collective-permute-done.6.refs_8_ = bf16[128,384]{1,0:T(8,128)(2,1)S(1)} collective-permute-done((bf16[128,384]{1,0:T(8,128)(2,1)S(1)}, bf16[128,384]{1,0:T(8,128)(2,1)S(1)}, u32[]{:S(2)}, u32[]{:S(2)}) %collective-permute-start.6) | collective-permute-done | bytes 98336 | tf_op jit(solution)/shard_map/ppermute | solution.py:25
  23.2 2.1 %collective-permute-done.5.refs_7_ = bf16[128,384]{1,0:T(8,128)(2,1)S(1)} collective-permute-done((bf16[128,384]{1,0:T(8,128)(2,1)S(1)}, bf16[128,384]{1,0:T(8,128)(2,1)S(1)}, u32[]{:S(2)}, u32[]{:S(2)}) %collective-permute-start.5) | collective-permute-done | bytes 98336 | tf_op jit(solution)/shard_map/ppermute | solution.py:25
  25.3 2.0 %collective-permute-done.7.refs_9_ = bf16[128,384]{1,0:T(8,128)(2,1)S(1)} collective-permute-done((bf16[128,384]{1,0:T(8,128)(2,1)S(1)}, bf16[128,384]{1,0:T(8,128)(2,1)S(1)}, u32[]{:S(2)}, u32[]{:S(2)}) %collective-permute-start.7) | collective-permute-done | bytes 98336 | tf_op jit(solution)/shard_map/ppermute | solution.py:25
  28.9 1.9 %collective-permute-start.19 = (bf16[128,512]{1,0:T(8,128)(2,1)S(1)}, bf16[128,512]{1,0:T(8,128)(2,1)S(1)}, u32[]{:S(2)}, u32[]{:S(2)}) collective-permute-start(bf16[128,512]{1,0:T(8,128)(2,1)S(1)} %constant_dynamic-slice_fusion.refs_4_), channel_id=1, source_target_pairs={{0,6},{1,7},{2,4},{3,5},{4,2},{5,3},{6,0},{7,1},{8,14},{9,15},{10,... | collective-permute-start | bytes 393224 | tf_op jit(solution)/shard_map/ppermute | solution.py:25
  34.3 3.9 %collective-permute-done.17.refs_8_ = bf16[128,512]{1,0:T(8,128)(2,1)S(1)} collective-permute-done((bf16[128,512]{1,0:T(8,128)(2,1)S(1)}, bf16[128,512]{1,0:T(8,128)(2,1)S(1)}, u32[]{:S(2)}, u32[]{:S(2)}) %collective-permute-start.17) | collective-permute-done | bytes 131104 | tf_op jit(solution)/shard_map/ppermute | solution.py:25
  46.8 2.7 %collective-permute-done.12 = bf16[256,256]{1,0:T(8,128)(2,1)S(1)} collective-permute-done((bf16[256,256]{1,0:T(8,128)(2,1)S(1)}, bf16[256,256]{1,0:T(8,128)(2,1)S(1)}, u32[]{:S(2)}, u32[]{:S(2)}) %collective-permute-start.12) | collective-permute-done | bytes 131104 | tf_op jit(solution)/shard_map/ppermute | solution.py:25
  51.4 2.2 %shard_map.124 = (bf16[128,1024]{1,0:T(8,128)(2,1)}, f32[128,128]{1,0:T(8,128)S(1)}, bf16[48,1024]{1,0:T(8,128)(2,1)S(1)}, bf16[48,1024]{1,0:T(8,128)(2,1)S(1)},...) custom-call(s32[3]{0:T(128)S(1)} %pad_add_fusion.place, ...), custom_call_target="tpu_custom_call" | custom-call | flops 369098752 | bytes 3757068 | tf_op jit(solution)/shard_map/pallas_call | solution.py:32
  56.6 3.0 %collective-permute-start.32 = (bf16[48,1024]{1,0:T(8,128)(2,1)S(1)}, bf16[48,1024]{1,0:T(8,128)(2,1)S(1)}, u32[]{:S(2)}, u32[]{:S(2)}) collective-permute-start(bf16[48,1024]{1,0:T(8,128)(2,1)S(1)} %get-tuple-element.61), channel_id=1, source_target_pairs={{0,7},{1,6},{2,5},{3,4},{4,3},{5,2},{6,1},{7,0},{8,15},{9,14},{10,... | collective-permute-start | bytes 294920 | tf_op jit(solution)/shard_map/ppermute | solution.py:25
  59.6 1.7 %collective-permute-start.29 = (bf16[48,1024]{1,0:T(8,128)(2,1)S(1)}, bf16[48,1024]{1,0:T(8,128)(2,1)S(1)}, u32[]{:S(2)}, u32[]{:S(2)}) collective-permute-start(bf16[48,1024]{1,0:T(8,128)(2,1)S(1)} %get-tuple-element.57), channel_id=1, source_target_pairs={{0,6},{1,7},{2,4},{3,5},{4,2},{5,3},{6,0},{7,1},{8,14},{9,15},{10,... | collective-permute-start | bytes 294920 | tf_op jit(solution)/shard_map/ppermute | solution.py:25
  61.3 6.6 %collective-permute-done.30 = bf16[48,1024]{1,0:T(8,128)(2,1)S(1)} collective-permute-done((bf16[48,1024]{1,0:T(8,128)(2,1)S(1)}, bf16[48,1024]{1,0:T(8,128)(2,1)S(1)}, u32[]{:S(2)}, u32[]{:S(2)}) %collective-permute-start.30) | collective-permute-done | bytes 98336 | tf_op jit(solution)/shard_map/ppermute | solution.py:25
  67.9 2.8 %collective-permute-done.31 = bf16[48,1024]{1,0:T(8,128)(2,1)S(1)} collective-permute-done((bf16[48,1024]{1,0:T(8,128)(2,1)S(1)}, bf16[48,1024]{1,0:T(8,128)(2,1)S(1)}, u32[]{:S(2)}, u32[]{:S(2)}) %collective-permute-start.31) | collective-permute-done | bytes 98336 | tf_op jit(solution)/shard_map/ppermute | solution.py:25
  75.4 3.9 %collective-permute-done.42.refs_1_ = bf16[96,1024]{1,0:T(8,128)(2,1)S(1)} collective-permute-done((bf16[96,1024]{1,0:T(8,128)(2,1)S(1)}, bf16[96,1024]{1,0:T(8,128)(2,1)S(1)}, u32[]{:S(2)}, u32[]{:S(2)}) %collective-permute-start.42) | collective-permute-done | bytes 196640 | tf_op jit(solution)/shard_map/ppermute | solution.py:25
  80.8 4.2 %shard_map.125 = (bf16[96,1024]{1,0:T(8,128)(2,1)S(1)}, bf16[96,1024]{1,0:T(8,128)(2,1)S(1)}, bf16[96,1024]{1,0:T(8,128)(2,1)S(1)}, bf16[96,1024]{1,0:T(8,128)(2,1)S(1)}) custom-call(bf16[96,1024]{1,0:T(8,128)(2,1)S(1)} %constant_dynamic-update-slice_fusion.refs_0_, bf16[96,1024]{1,0:T(8,128)(2,1)S(1)} %collective-permute-done.42.refs_1_, ...), custom_call_target="tpu_custom_call" | custom-call | flops 2415919104 | bytes 7864320 | tf_op jit(solution)/shard_map/pallas_call | solution.py:32
  86.1 4.8 %collective-permute-done.36.refs_1_ = bf16[192,1024]{1,0:T(8,128)(2,1)S(1)} collective-permute-done((bf16[192,1024]{1,0:T(8,128)(2,1)S(1)}, bf16[192,1024]{1,0:T(8,128)(2,1)S(1)}, u32[]{:S(2)}, u32[]{:S(2)}) %collective-permute-start.36) | collective-permute-done | bytes 393248 | tf_op jit(solution)/shard_map/ppermute | solution.py:25
  92.2 4.2 %shard_map.128 = (bf16[96,1024]{1,0:T(8,128)(2,1)S(1)}, bf16[96,1024]{1,0:T(8,128)(2,1)S(1)}, bf16[96,1024]{1,0:T(8,128)(2,1)S(1)}, bf16[96,1024]{1,0:T(8,128)(2,1)S(1)}) custom-call(bf16[96,1024]{1,0:T(8,128)(2,1)S(1)} %constant_dynamic-update-slice_fusion.2.refs_0_, bf16[96,1024]{1,0:T(8,128)(2,1)S(1)} %collective-permute-done.39.refs_1_, ...), custom_call_target="tpu_custom_call" | custom-call | flops 2415919104 | bytes 7864320 | tf_op jit(solution)/shard_map/pallas_call | solution.py:32
  98.6 7.5 %shard_map.132 = (bf16[192,1024]{1,0:T(8,128)(2,1)S(1)}, bf16[192,1024]{1,0:T(8,128)(2,1)S(1)}, bf16[192,1024]{1,0:T(8,128)(2,1)S(1)}, bf16[192,1024]{1,0:T(8,128)(2,1)S(1)}) custom-call(bf16[192,1024]{1,0:T(8,128)(2,1)S(1)} %constant_dynamic-update-slice_fusion.4.refs_0_, bf16[192,1024]{1,0:T(8,128)(2,1)S(1)} %collective-permute-done.36.refs_1_, ...), custom_call_target="tpu_custom_call" | custom-call | flops 4831838208 | bytes 9437184 | tf_op jit(solution)/shard_map/pallas_call | solution.py:32
  110.0 2.2 %collective-permute-start.56 = (bf16[48,1024]{1,0:T(8,128)(2,1)S(1)}, bf16[48,1024]{1,0:T(8,128)(2,1)S(1)}, u32[]{:S(2)}, u32[]{:S(2)}) collective-permute-start(bf16[48,1024]{1,0:T(8,128)(2,1)S(1)} %get-tuple-element.82), channel_id=1, source_target_pairs={{0,4},{1,5},{2,6},{3,7},{4,0},{5,1},{6,2},{7,3},{8,12},{9,13},{10,... | collective-permute-start | bytes 294920 | tf_op jit(solution)/shard_map/ppermute | solution.py:25
  113.5 9.8 %collective-permute-done.58.refs_1_ = bf16[96,1024]{1,0:T(8,128)(2,1)S(1)} collective-permute-done((bf16[96,1024]{1,0:T(8,128)(2,1)S(1)}, bf16[96,1024]{1,0:T(8,128)(2,1)S(1)}, u32[]{:S(2)}, u32[]{:S(2)}) %collective-permute-start.58) | collective-permute-done | bytes 196640 | tf_op jit(solution)/shard_map/ppermute | solution.py:25
  123.4 2.6 %collective-permute-start.59 = (bf16[48,1024]{1,0:T(8,128)(2,1)S(1)}, bf16[48,1024]{1,0:T(8,128)(2,1)S(1)}, u32[]{:S(2)}, u32[]{:S(2)}) collective-permute-start(bf16[48,1024]{1,0:T(8,128)(2,1)S(1)} %get-tuple-element.96), channel_id=1, source_target_pairs={{0,6},{1,7},{2,4},{3,5},{4,2},{5,3},{6,0},{7,1},{8,14},{9,15},{10,... | collective-permute-start | bytes 294920 | tf_op jit(solution)/shard_map/ppermute | solution.py:25
  126.0 1.9 %collective-permute-start.60 = (bf16[48,1024]{1,0:T(8,128)(2,1)S(1)}, bf16[48,1024]{1,0:T(8,128)(2,1)S(1)}, u32[]{:S(2)}, u32[]{:S(2)}) collective-permute-start(bf16[48,1024]{1,0:T(8,128)(2,1)S(1)} %get-tuple-element.97), channel_id=1, source_target_pairs={{0,7},{1,6},{2,5},{3,4},{4,3},{5,2},{6,1},{7,0},{8,15},{9,14},{10,... | collective-permute-start | bytes 294920 | tf_op jit(solution)/shard_map/ppermute | solution.py:25
  129.1 2.6 %collective-permute-start.55 = (bf16[48,1024]{1,0:T(8,128)(2,1)S(1)}, bf16[48,1024]{1,0:T(8,128)(2,1)S(1)}, u32[]{:S(2)}, u32[]{:S(2)}) collective-permute-start(bf16[48,1024]{1,0:T(8,128)(2,1)S(1)} %get-tuple-element.95), channel_id=1, source_target_pairs={{0,3},{1,2},{2,1},{3,0},{4,7},{5,6},{6,5},{7,4},{8,11},{9,10},{10,... | collective-permute-start | bytes 294920 | tf_op jit(solution)/shard_map/ppermute | solution.py:25
  131.7 2.4 %collective-permute-done.60.refs_8_ = bf16[48,1024]{1,0:T(8,128)(2,1)S(1)} collective-permute-done((bf16[48,1024]{1,0:T(8,128)(2,1)S(1)}, bf16[48,1024]{1,0:T(8,128)(2,1)S(1)}, u32[]{:S(2)}, u32[]{:S(2)}) %collective-permute-start.60) | collective-permute-done | bytes 98336 | tf_op jit(solution)/shard_map/ppermute | solution.py:25
  (148 shorter events, 50.3 us)
Async XLA Ops:
  2.9 10.9 %collective-permute-start.1 = (bf16[128,1024]{1,0:T(8,128)(2,1)S(1)}, bf16[128,1024]{1,0:T(8,128)(2,1)S(1)}, u32[]{:S(2)}, u32[]{:S(2)}) collective-permute-start(bf16[128,1024]{1,0:T(8,128)(2,1)S(1)} %fusion.2.refs_0_), channel_id=1, source_target_pairs={{0,16},{8,24},{16,0},{24,8},{1,17},{9,25},{17,1},{25,9},{2,18},{10... | collective-permute-start | bytes 786440 | tf_op jit(solution)/shard_map/ppermute | solution.py:25
  9.2 21.7 %collective-permute-start = (bf16[128,1024]{1,0:T(8,128)(2,1)S(1)}, bf16[128,1024]{1,0:T(8,128)(2,1)S(1)}, u32[]{:S(2)}, u32[]{:S(2)}) collective-permute-start(bf16[128,1024]{1,0:T(8,128)(2,1)S(1)} %fusion.2.refs_0_), channel_id=1, source_target_pairs={{0,8},{8,0},{16,24},{24,16},{1,9},{9,1},{17,25},{25,17},{2,10},{10... | collective-permute-start | bytes 786440 | tf_op jit(solution)/shard_map/ppermute | solution.py:25
  9.2 10.4 %collective-permute-start.6 = (bf16[128,384]{1,0:T(8,128)(2,1)S(1)}, bf16[128,384]{1,0:T(8,128)(2,1)S(1)}, u32[]{:S(2)}, u32[]{:S(2)}) collective-permute-start(bf16[128,384]{1,0:T(8,128)(2,1)S(1)} %pad_maximum_fusion.refs_4_), channel_id=1, source_target_pairs={{0,4},{1,5},{2,6},{3,7},{4,0},{5,1},{6,2},{7,3},{8,12},{9,13},{10,... | collective-permute-start | bytes 294920 | tf_op jit(solution)/shard_map/ppermute | solution.py:25
  11.8 9.4 %collective-permute-start.8 = (bf16[128,384]{1,0:T(8,128)(2,1)S(1)}, bf16[128,384]{1,0:T(8,128)(2,1)S(1)}, u32[]{:S(2)}, u32[]{:S(2)}) collective-permute-start(bf16[128,384]{1,0:T(8,128)(2,1)S(1)} %pad_maximum_fusion.refs_4_), channel_id=1, source_target_pairs={{0,6},{1,7},{2,4},{3,5},{4,2},{5,3},{6,0},{7,1},{8,14},{9,15},{10,... | collective-permute-start | bytes 294920 | tf_op jit(solution)/shard_map/ppermute | solution.py:25
  12.2 9.4 %collective-permute-start.3 = (bf16[128,384]{1,0:T(8,128)(2,1)S(1)}, bf16[128,384]{1,0:T(8,128)(2,1)S(1)}, u32[]{:S(2)}, u32[]{:S(2)}) collective-permute-start(bf16[128,384]{1,0:T(8,128)(2,1)S(1)} %pad_maximum_fusion.refs_4_), channel_id=1, source_target_pairs={{0,1},{1,0},{2,3},{3,2},{4,5},{5,4},{6,7},{7,6},{8,9},{9,8},{10,11... | collective-permute-start | bytes 294920 | tf_op jit(solution)/shard_map/ppermute | solution.py:25
  13.8 18.5 %collective-permute-start.2 = (bf16[128,1024]{1,0:T(8,128)(2,1)S(1)}, bf16[128,1024]{1,0:T(8,128)(2,1)S(1)}, u32[]{:S(2)}, u32[]{:S(2)}) collective-permute-start(bf16[128,1024]{1,0:T(8,128)(2,1)S(1)} %collective-permute-done.1.refs_2_), channel_id=1, source_target_pairs={{0,8},{8,0},{16,24},{24,16},{1,9},{9,1},{17,25},{25,17},{2,10},{10... | collective-permute-start | bytes 786440 | tf_op jit(solution)/shard_map/ppermute | solution.py:25
  25.3 8.5 %collective-permute-start.15 = (bf16[128,512]{1,0:T(8,128)(2,1)S(1)}, bf16[128,512]{1,0:T(8,128)(2,1)S(1)}, u32[]{:S(2)}, u32[]{:S(2)}) collective-permute-start(bf16[128,512]{1,0:T(8,128)(2,1)S(1)} %constant_dynamic-slice_fusion.refs_4_), channel_id=1, source_target_pairs={{0,2},{1,3},{2,0},{3,1},{4,6},{5,7},{6,4},{7,5},{8,10},{9,11},{10,... | collective-permute-start | bytes 393224 | tf_op jit(solution)/shard_map/ppermute | solution.py:25
  27.3 10.9 %collective-permute-start.17 = (bf16[128,512]{1,0:T(8,128)(2,1)S(1)}, bf16[128,512]{1,0:T(8,128)(2,1)S(1)}, u32[]{:S(2)}, u32[]{:S(2)}) collective-permute-start(bf16[128,512]{1,0:T(8,128)(2,1)S(1)} %constant_dynamic-slice_fusion.refs_4_), channel_id=1, source_target_pairs={{0,4},{1,5},{2,6},{3,7},{4,0},{5,1},{6,2},{7,3},{8,12},{9,13},{10,... | collective-permute-start | bytes 393224 | tf_op jit(solution)/shard_map/ppermute | solution.py:25
  28.9 10.8 %collective-permute-start.19 = (bf16[128,512]{1,0:T(8,128)(2,1)S(1)}, bf16[128,512]{1,0:T(8,128)(2,1)S(1)}, u32[]{:S(2)}, u32[]{:S(2)}) collective-permute-start(bf16[128,512]{1,0:T(8,128)(2,1)S(1)} %constant_dynamic-slice_fusion.refs_4_), channel_id=1, source_target_pairs={{0,6},{1,7},{2,4},{3,5},{4,2},{5,3},{6,0},{7,1},{8,14},{9,15},{10,... | collective-permute-start | bytes 393224 | tf_op jit(solution)/shard_map/ppermute | solution.py:25
  30.9 9.4 %collective-permute-start.14 = (bf16[128,512]{1,0:T(8,128)(2,1)S(1)}, bf16[128,512]{1,0:T(8,128)(2,1)S(1)}, u32[]{:S(2)}, u32[]{:S(2)}) collective-permute-start(bf16[128,512]{1,0:T(8,128)(2,1)S(1)} %constant_dynamic-slice_fusion.refs_4_), channel_id=1, source_target_pairs={{0,1},{1,0},{2,3},{3,2},{4,5},{5,4},{6,7},{7,6},{8,9},{9,8},{10,11... | collective-permute-start | bytes 393224 | tf_op jit(solution)/shard_map/ppermute | solution.py:25
  33.8 9.6 %collective-permute-start.21 = (bf16[128,512]{1,0:T(8,128)(2,1)S(1)}, bf16[128,512]{1,0:T(8,128)(2,1)S(1)}, u32[]{:S(2)}, u32[]{:S(2)}) collective-permute-start(bf16[128,512]{1,0:T(8,128)(2,1)S(1)} %constant_dynamic-slice_fusion.refs_4_), channel_id=1, source_target_pairs={{0,8},{8,0},{16,24},{24,16},{1,9},{9,1},{17,25},{25,17},{2,10},{10... | collective-permute-start | bytes 393224 | tf_op jit(solution)/shard_map/ppermute | solution.py:25
  53.6 14.3 %collective-permute-start.30 = (bf16[48,1024]{1,0:T(8,128)(2,1)S(1)}, bf16[48,1024]{1,0:T(8,128)(2,1)S(1)}, u32[]{:S(2)}, u32[]{:S(2)}) collective-permute-start(bf16[48,1024]{1,0:T(8,128)(2,1)S(1)} %get-tuple-element.58), channel_id=1, source_target_pairs={{0,4},{1,5},{2,6},{3,7},{4,0},{5,1},{6,2},{7,3},{8,12},{9,13},{10,... | collective-permute-start | bytes 294920 | tf_op jit(solution)/shard_map/ppermute | solution.py:25
  55.2 15.6 %collective-permute-start.31 = (bf16[48,1024]{1,0:T(8,128)(2,1)S(1)}, bf16[48,1024]{1,0:T(8,128)(2,1)S(1)}, u32[]{:S(2)}, u32[]{:S(2)}) collective-permute-start(bf16[48,1024]{1,0:T(8,128)(2,1)S(1)} %get-tuple-element.59), channel_id=1, source_target_pairs={{0,5},{1,4},{2,7},{3,6},{4,1},{5,0},{6,3},{7,2},{8,13},{9,12},{10,... | collective-permute-start | bytes 294920 | tf_op jit(solution)/shard_map/ppermute | solution.py:25
  56.6 14.9 %collective-permute-start.32 = (bf16[48,1024]{1,0:T(8,128)(2,1)S(1)}, bf16[48,1024]{1,0:T(8,128)(2,1)S(1)}, u32[]{:S(2)}, u32[]{:S(2)}) collective-permute-start(bf16[48,1024]{1,0:T(8,128)(2,1)S(1)} %get-tuple-element.61), channel_id=1, source_target_pairs={{0,7},{1,6},{2,5},{3,4},{4,3},{5,2},{6,1},{7,0},{8,15},{9,14},{10,... | collective-permute-start | bytes 294920 | tf_op jit(solution)/shard_map/ppermute | solution.py:25
  59.6 12.5 %collective-permute-start.29 = (bf16[48,1024]{1,0:T(8,128)(2,1)S(1)}, bf16[48,1024]{1,0:T(8,128)(2,1)S(1)}, u32[]{:S(2)}, u32[]{:S(2)}) collective-permute-start(bf16[48,1024]{1,0:T(8,128)(2,1)S(1)} %get-tuple-element.57), channel_id=1, source_target_pairs={{0,6},{1,7},{2,4},{3,5},{4,2},{5,3},{6,0},{7,1},{8,14},{9,15},{10,... | collective-permute-start | bytes 294920 | tf_op jit(solution)/shard_map/ppermute | solution.py:25
  61.3 10.8 %collective-permute-start.35 = (bf16[48,1024]{1,0:T(8,128)(2,1)S(1)}, bf16[48,1024]{1,0:T(8,128)(2,1)S(1)}, u32[]{:S(2)}, u32[]{:S(2)}) collective-permute-start(bf16[48,1024]{1,0:T(8,128)(2,1)S(1)} %get-tuple-element.68), channel_id=1, source_target_pairs={{0,3},{1,2},{2,1},{3,0},{4,7},{5,6},{6,5},{7,4},{8,11},{9,10},{10,... | collective-permute-start | bytes 294920 | tf_op jit(solution)/shard_map/ppermute | solution.py:25
  72.1 13.6 %collective-permute-start.39 = (bf16[96,1024]{1,0:T(8,128)(2,1)S(1)}, bf16[96,1024]{1,0:T(8,128)(2,1)S(1)}, u32[]{:S(2)}, u32[]{:S(2)}) collective-permute-start(bf16[96,1024]{1,0:T(8,128)(2,1)S(1)} %constant_dynamic-update-slice_fusion.2.refs_0_), channel_id=1, source_target_pairs={{0,16},{8,24},{16,0},{24,8},{1,17},{9,25},{17,1},{25,9},{2,18},{10... | collective-permute-start | bytes 589832 | tf_op jit(solution)/shard_map/ppermute | solution.py:25
  79.3 11.6 %collective-permute-start.36 = (bf16[192,1024]{1,0:T(8,128)(2,1)S(1)}, bf16[192,1024]{1,0:T(8,128)(2,1)S(1)}, u32[]{:S(2)}, u32[]{:S(2)}) collective-permute-start(bf16[192,1024]{1,0:T(8,128)(2,1)S(1)} %constant_dynamic-update-slice_fusion.4.refs_0_), channel_id=1, source_target_pairs={{0,16},{8,24},{16,0},{24,8},{1,17},{9,25},{17,1},{25,9},{2,18},{10... | collective-permute-start | bytes 1179656 | tf_op jit(solution)/shard_map/ppermute | solution.py:25
  106.1 19.9 %collective-permute-start.50 = (bf16[192,1024]{1,0:T(8,128)(2,1)S(1)}, bf16[192,1024]{1,0:T(8,128)(2,1)S(1)}, u32[]{:S(2)}, u32[]{:S(2)}) collective-permute-start(bf16[192,1024]{1,0:T(8,128)(2,1)S(1)} %get-tuple-element.89), channel_id=1, source_target_pairs={{0,8},{8,0},{16,24},{24,16},{1,9},{9,1},{17,25},{25,17},{2,10},{10... | collective-permute-start | bytes 1179656 | tf_op jit(solution)/shard_map/ppermute | solution.py:25
  107.9 20.1 %collective-permute-start.52 = (bf16[192,1024]{1,0:T(8,128)(2,1)S(1)}, bf16[192,1024]{1,0:T(8,128)(2,1)S(1)}, u32[]{:S(2)}, u32[]{:S(2)}) collective-permute-start(bf16[192,1024]{1,0:T(8,128)(2,1)S(1)} %shard_map.134), channel_id=1, source_target_pairs={{0,16},{8,24},{16,0},{24,8},{1,17},{9,25},{17,1},{25,9},{2,18},{10... | collective-permute-start | bytes 1179656 | tf_op jit(solution)/shard_map/ppermute | solution.py:25
  109.2 14.2 %collective-permute-start.58 = (bf16[96,1024]{1,0:T(8,128)(2,1)S(1)}, bf16[96,1024]{1,0:T(8,128)(2,1)S(1)}, u32[]{:S(2)}, u32[]{:S(2)}) collective-permute-start(bf16[96,1024]{1,0:T(8,128)(2,1)S(1)} %shard_map.129), channel_id=1, source_target_pairs={{0,16},{8,24},{16,0},{24,8},{1,17},{9,25},{17,1},{25,9},{2,18},{10... | collective-permute-start | bytes 589832 | tf_op jit(solution)/shard_map/ppermute | solution.py:25
  110.0 19.0 %collective-permute-start.56 = (bf16[48,1024]{1,0:T(8,128)(2,1)S(1)}, bf16[48,1024]{1,0:T(8,128)(2,1)S(1)}, u32[]{:S(2)}, u32[]{:S(2)}) collective-permute-start(bf16[48,1024]{1,0:T(8,128)(2,1)S(1)} %get-tuple-element.82), channel_id=1, source_target_pairs={{0,4},{1,5},{2,6},{3,7},{4,0},{5,1},{6,2},{7,3},{8,12},{9,13},{10,... | collective-permute-start | bytes 294920 | tf_op jit(solution)/shard_map/ppermute | solution.py:25
  112.3 16.8 %collective-permute-start.57 = (bf16[48,1024]{1,0:T(8,128)(2,1)S(1)}, bf16[48,1024]{1,0:T(8,128)(2,1)S(1)}, u32[]{:S(2)}, u32[]{:S(2)}) collective-permute-start(bf16[48,1024]{1,0:T(8,128)(2,1)S(1)} %get-tuple-element.83), channel_id=1, source_target_pairs={{0,5},{1,4},{2,7},{3,6},{4,1},{5,0},{6,3},{7,2},{8,13},{9,12},{10,... | collective-permute-start | bytes 294920 | tf_op jit(solution)/shard_map/ppermute | solution.py:25
  123.4 8.2 %collective-permute-start.59 = (bf16[48,1024]{1,0:T(8,128)(2,1)S(1)}, bf16[48,1024]{1,0:T(8,128)(2,1)S(1)}, u32[]{:S(2)}, u32[]{:S(2)}) collective-permute-start(bf16[48,1024]{1,0:T(8,128)(2,1)S(1)} %get-tuple-element.96), channel_id=1, source_target_pairs={{0,6},{1,7},{2,4},{3,5},{4,2},{5,3},{6,0},{7,1},{8,14},{9,15},{10,... | collective-permute-start | bytes 294920 | tf_op jit(solution)/shard_map/ppermute | solution.py:25
  (44 other events, 451.0 us)

commit v3 on v2

--- a/solution.py
+++ b/solution.py
@@ -253,7 +253,6 @@
     place = jnp.stack([me, core, ctx]).astype(jnp.int32)
     heads = w_query.shape[1] // HD // lax.axis_size("ctx")
 
-    attn_in = (rms_scaled(inputs.astype(F32)) * attn_gain).astype(BF16)
     piece = jnp.concatenate(
         [
             lax.dynamic_slice_in_dim(w_query, ctx * heads * HD, heads * HD, 1),
@@ -262,6 +261,8 @@
         axis=1,
     )
     weights = gather(piece, small)
+    held = after(inputs, piece) if small else inputs
+    attn_in = (rms_scaled(held.astype(F32)) * attn_gain).astype(BF16)
     near = swap(attn_in, "ctx", 1)
     far = swap(attn_in, "ctx", 2)
     across = swap(far, "ctx", 1)
@@ -345,8 +346,10 @@
         earlier = own
     returned = {}
     earlier, waiting = None, None
+    xs, rets = [], []
     for group, own in zip(groups, owns):
-        from_x = swap(own, "ctx", 2)
+        from_x = swap(after(own, xs[-2]) if len(xs) > 1 else own, "ctx", 2)
+        xs.append(from_x)
         from_core = swap(own, "ctx", 1)
         from_both = swap(from_x, "ctx", 1)
         taken = [own, from_x, from_core, from_both]
@@ -367,7 +370,8 @@
         core_x = swap(terms[3], "ctx", 1)
         core_own = swap(terms[2], "ctx", 1)
         (sum_x,) = add([terms[1]], [core_x], 1)
-        x_own = swap(sum_x, "ctx", 2)
+        x_own = swap(after(sum_x, rets[-1]) if rets else sum_x, "ctx", 2)
+        rets.append(x_own)
         (sum_own,) = add([terms[0]], [core_own], 1)
         final = add([sum_own], [x_own], len(group))
         earlier = [sum_x, sum_own] + (waiting or [])

time: 138 us -> 137 us (level)
  starting transfers between devices: 52 us -> 47.9 us
  waiting for transfers between devices: 57.8 us -> 60.3 us
    ppermute x61, starting transfers between devices: 52 us -> 47.9 us  [swap(): return lax.ppermute(value, axis, [(i, i ^ bits) for i in range(size)])]
    ppermute x61, waiting for transfers between devices: 57.8 us -> 60.3 us  [swap(): return lax.ppermute(value, axis, [(i, i ^ bits) for i in range(size)])]
  transfers between devices with their start and end apart: 61 -> 61, of which waited for: 24 -> 30; matrix products, arithmetic and copies ran while one was open for 1% -> 0% of each run, Pallas kernels for 9% -> 9%
where the time goes in v3:
time: 137 us
  waiting for transfers between devices  60.3 us (44%)
  starting transfers between devices  47.9 us (35%)
  Pallas kernels  23 us (17%)
  other arithmetic  2.26 us (2%)
  local copies, waits for them, and re-layouts  2.06 us (2%)
    ppermute x61, waiting for transfers between devices, swap(): return lax.ppermute(value, axis, [(i, i ^ bits) for i in range(size)])  60.3 us
    ppermute x61, starting transfers between devices, swap(): return lax.ppermute(value, axis, [(i, i ^ bits) for i in range(size)])  47.9 us
    pallas_call x16, Pallas kernels, call(): pl.pallas_call(kernel, out_shape=outs, in_specs=[SMEM] + [VMEM] * (len(ar...  23 us
  transfers between devices with their start and end apart: 61, of which 30 were waited for; matrix products, arithmetic and copies ran while one was open for 0% of the time, Pallas kernels for 9%

profile of v3, /device:TPU:0, one launch (start us, length us, event | category | flops | bytes accessed | tf_op | source)
XLA Modules:
  0.0 136.5 jit_solution(17961368025150196864)
XLA Ops:
  4.6 3.0 %collective-permute-start.1 = (bf16[128,1024]{1,0:T(8,128)(2,1)S(1)}, bf16[128,1024]{1,0:T(8,128)(2,1)S(1)}, u32[]{:S(2)}, u32[]{:S(2)}) collective-permute-start(bf16[128,1024]{1,0:T(8,128)(2,1)S(1)} %fusion.2.refs_0_), channel_id=1, source_target_pairs={{0,16},{8,24},{16,0},{24,8},{1,17},{9,25},{17,1},{25,9},{2,18},{10... | collective-permute-start | bytes 786440 | tf_op jit(solution)/shard_map/ppermute | solution.py:25
  9.1 2.6 %collective-permute-start.6 = (bf16[128,384]{1,0:T(8,128)(2,1)S(1)}, bf16[128,384]{1,0:T(8,128)(2,1)S(1)}, u32[]{:S(2)}, u32[]{:S(2)}) collective-permute-start(bf16[128,384]{1,0:T(8,128)(2,1)S(1)} %pad_maximum_fusion.refs_4_), channel_id=1, source_target_pairs={{0,4},{1,5},{2,6},{3,7},{4,0},{5,1},{6,2},{7,3},{8,12},{9,13},{10,... | collective-permute-start | bytes 294920 | tf_op jit(solution)/shard_map/ppermute | solution.py:25
  13.9 5.7 %collective-permute-done.6.refs_8_ = bf16[128,384]{1,0:T(8,128)(2,1)S(1)} collective-permute-done((bf16[128,384]{1,0:T(8,128)(2,1)S(1)}, bf16[128,384]{1,0:T(8,128)(2,1)S(1)}, u32[]{:S(2)}, u32[]{:S(2)}) %collective-permute-start.6) | collective-permute-done | bytes 98336 | tf_op jit(solution)/shard_map/ppermute | solution.py:25
  23.1 2.1 %collective-permute-done.5.refs_7_ = bf16[128,384]{1,0:T(8,128)(2,1)S(1)} collective-permute-done((bf16[128,384]{1,0:T(8,128)(2,1)S(1)}, bf16[128,384]{1,0:T(8,128)(2,1)S(1)}, u32[]{:S(2)}, u32[]{:S(2)}) %collective-permute-start.5) | collective-permute-done | bytes 98336 | tf_op jit(solution)/shard_map/ppermute | solution.py:25
  25.2 2.0 %collective-permute-done.7.refs_9_ = bf16[128,384]{1,0:T(8,128)(2,1)S(1)} collective-permute-done((bf16[128,384]{1,0:T(8,128)(2,1)S(1)}, bf16[128,384]{1,0:T(8,128)(2,1)S(1)}, u32[]{:S(2)}, u32[]{:S(2)}) %collective-permute-start.7) | collective-permute-done | bytes 98336 | tf_op jit(solution)/shard_map/ppermute | solution.py:25
  34.3 3.9 %collective-permute-done.17.refs_8_ = bf16[128,512]{1,0:T(8,128)(2,1)S(1)} collective-permute-done((bf16[128,512]{1,0:T(8,128)(2,1)S(1)}, bf16[128,512]{1,0:T(8,128)(2,1)S(1)}, u32[]{:S(2)}, u32[]{:S(2)}) %collective-permute-start.17) | collective-permute-done | bytes 131104 | tf_op jit(solution)/shard_map/ppermute | solution.py:25
  46.8 2.7 %collective-permute-done.12 = bf16[256,256]{1,0:T(8,128)(2,1)S(1)} collective-permute-done((bf16[256,256]{1,0:T(8,128)(2,1)S(1)}, bf16[256,256]{1,0:T(8,128)(2,1)S(1)}, u32[]{:S(2)}, u32[]{:S(2)}) %collective-permute-start.12) | collective-permute-done | bytes 131104 | tf_op jit(solution)/shard_map/ppermute | solution.py:25
  51.3 2.2 %shard_map.124 = (bf16[128,1024]{1,0:T(8,128)(2,1)}, f32[128,128]{1,0:T(8,128)S(1)}, bf16[48,1024]{1,0:T(8,128)(2,1)S(1)}, bf16[48,1024]{1,0:T(8,128)(2,1)S(1)},...) custom-call(s32[3]{0:T(128)S(1)} %pad_add_fusion.place, ...), custom_call_target="tpu_custom_call" | custom-call | flops 369098752 | bytes 3757068 | tf_op jit(solution)/shard_map/pallas_call | solution.py:32
  56.5 3.0 %collective-permute-start.32 = (bf16[48,1024]{1,0:T(8,128)(2,1)S(1)}, bf16[48,1024]{1,0:T(8,128)(2,1)S(1)}, u32[]{:S(2)}, u32[]{:S(2)}) collective-permute-start(bf16[48,1024]{1,0:T(8,128)(2,1)S(1)} %get-tuple-element.66), channel_id=1, source_target_pairs={{0,7},{1,6},{2,5},{3,4},{4,3},{5,2},{6,1},{7,0},{8,15},{9,14},{10,... | collective-permute-start | bytes 294920 | tf_op jit(solution)/shard_map/ppermute | solution.py:25
  61.3 6.6 %collective-permute-done.30 = bf16[48,1024]{1,0:T(8,128)(2,1)S(1)} collective-permute-done((bf16[48,1024]{1,0:T(8,128)(2,1)S(1)}, bf16[48,1024]{1,0:T(8,128)(2,1)S(1)}, u32[]{:S(2)}, u32[]{:S(2)}) %collective-permute-start.30) | collective-permute-done | bytes 98336 | tf_op jit(solution)/shard_map/ppermute | solution.py:25
  67.9 2.8 %collective-permute-done.31 = bf16[48,1024]{1,0:T(8,128)(2,1)S(1)} collective-permute-done((bf16[48,1024]{1,0:T(8,128)(2,1)S(1)}, bf16[48,1024]{1,0:T(8,128)(2,1)S(1)}, u32[]{:S(2)}, u32[]{:S(2)}) %collective-permute-start.31) | collective-permute-done | bytes 98336 | tf_op jit(solution)/shard_map/ppermute | solution.py:25
  75.3 3.9 %collective-permute-done.36.refs_1_ = bf16[96,1024]{1,0:T(8,128)(2,1)S(1)} collective-permute-done((bf16[96,1024]{1,0:T(8,128)(2,1)S(1)}, bf16[96,1024]{1,0:T(8,128)(2,1)S(1)}, u32[]{:S(2)}, u32[]{:S(2)}) %collective-permute-start.36) | collective-permute-done | bytes 196640 | tf_op jit(solution)/shard_map/ppermute | solution.py:25
  80.7 4.2 %shard_map.125 = (bf16[96,1024]{1,0:T(8,128)(2,1)S(1)}, bf16[96,1024]{1,0:T(8,128)(2,1)S(1)}, bf16[96,1024]{1,0:T(8,128)(2,1)S(1)}, bf16[96,1024]{1,0:T(8,128)(2,1)S(1)}) custom-call(bf16[96,1024]{1,0:T(8,128)(2,1)S(1)} %constant_dynamic-update-slice_fusion.refs_0_, bf16[96,1024]{1,0:T(8,128)(2,1)S(1)} %collective-permute-done.36.refs_1_, ...), custom_call_target="tpu_custom_call" | custom-call | flops 2415919104 | bytes 7864320 | tf_op jit(solution)/shard_map/pallas_call | solution.py:32
  87.6 3.7 %collective-permute-done.37.refs_1_ = bf16[192,1024]{1,0:T(8,128)(2,1)S(1)} collective-permute-done((bf16[192,1024]{1,0:T(8,128)(2,1)S(1)}, bf16[192,1024]{1,0:T(8,128)(2,1)S(1)}, u32[]{:S(2)}, u32[]{:S(2)}) %collective-permute-start.37) | collective-permute-done | bytes 393248 | tf_op jit(solution)/shard_map/ppermute | solution.py:25
  91.3 4.2 %shard_map.128 = (bf16[96,1024]{1,0:T(8,128)(2,1)S(1)}, bf16[96,1024]{1,0:T(8,128)(2,1)S(1)}, bf16[96,1024]{1,0:T(8,128)(2,1)S(1)}, bf16[96,1024]{1,0:T(8,128)(2,1)S(1)}) custom-call(bf16[96,1024]{1,0:T(8,128)(2,1)S(1)} %constant_dynamic-update-slice_fusion.2.refs_0_, bf16[96,1024]{1,0:T(8,128)(2,1)S(1)} %collective-permute-done.40.refs_1_, ...), custom_call_target="tpu_custom_call" | custom-call | flops 2415919104 | bytes 7864320 | tf_op jit(solution)/shard_map/pallas_call | solution.py:32
  97.6 7.5 %shard_map.132 = (bf16[192,1024]{1,0:T(8,128)(2,1)S(1)}, bf16[192,1024]{1,0:T(8,128)(2,1)S(1)}, bf16[192,1024]{1,0:T(8,128)(2,1)S(1)}, bf16[192,1024]{1,0:T(8,128)(2,1)S(1)}) custom-call(bf16[192,1024]{1,0:T(8,128)(2,1)S(1)} %constant_dynamic-update-slice_fusion.4.refs_0_, bf16[192,1024]{1,0:T(8,128)(2,1)S(1)} %collective-permute-done.37.refs_1_, ...), custom_call_target="tpu_custom_call" | custom-call | flops 4831838208 | bytes 9437184 | tf_op jit(solution)/shard_map/pallas_call | solution.py:32
  107.0 5.5 %collective-permute-done.52.refs_1_ = bf16[96,1024]{1,0:T(8,128)(2,1)S(1)} collective-permute-done((bf16[96,1024]{1,0:T(8,128)(2,1)S(1)}, bf16[96,1024]{1,0:T(8,128)(2,1)S(1)}, u32[]{:S(2)}, u32[]{:S(2)}) %collective-permute-start.52) | collective-permute-done | bytes 196640 | tf_op jit(solution)/shard_map/ppermute | solution.py:25
  116.3 2.3 %collective-permute-start.59 = (bf16[48,1024]{1,0:T(8,128)(2,1)S(1)}, bf16[48,1024]{1,0:T(8,128)(2,1)S(1)}, u32[]{:S(2)}, u32[]{:S(2)}) collective-permute-start(bf16[48,1024]{1,0:T(8,128)(2,1)S(1)} %get-tuple-element.104), channel_id=1, source_target_pairs={{0,6},{1,7},{2,4},{3,5},{4,2},{5,3},{6,0},{7,1},{8,14},{9,15},{10,... | collective-permute-start | bytes 294920 | tf_op jit(solution)/shard_map/ppermute | solution.py:25
  118.6 2.2 %collective-permute-start.60 = (bf16[48,1024]{1,0:T(8,128)(2,1)S(1)}, bf16[48,1024]{1,0:T(8,128)(2,1)S(1)}, u32[]{:S(2)}, u32[]{:S(2)}) collective-permute-start(bf16[48,1024]{1,0:T(8,128)(2,1)S(1)} %get-tuple-element.105), channel_id=1, source_target_pairs={{0,7},{1,6},{2,5},{3,4},{4,3},{5,2},{6,1},{7,0},{8,15},{9,14},{10,... | collective-permute-start | bytes 294920 | tf_op jit(solution)/shard_map/ppermute | solution.py:25
  120.8 2.0 %collective-permute-done.53.refs_1_ = bf16[192,1024]{1,0:T(8,128)(2,1)S(1)} collective-permute-done((bf16[192,1024]{1,0:T(8,128)(2,1)S(1)}, bf16[192,1024]{1,0:T(8,128)(2,1)S(1)}, u32[]{:S(2)}, u32[]{:S(2)}) %collective-permute-start.53) | collective-permute-done | bytes 393248 | tf_op jit(solution)/shard_map/ppermute | solution.py:25
  124.2 2.8 %collective-permute-done.57.refs_5_ = bf16[48,1024]{1,0:T(8,128)(2,1)S(1)} collective-permute-done((bf16[48,1024]{1,0:T(8,128)(2,1)S(1)}, bf16[48,1024]{1,0:T(8,128)(2,1)S(1)}, u32[]{:S(2)}, u32[]{:S(2)}) %collective-permute-start.57) | collective-permute-done | bytes 98336 | tf_op jit(solution)/shard_map/ppermute | solution.py:25
  127.0 2.8 %collective-permute-done.58.refs_6_ = bf16[48,1024]{1,0:T(8,128)(2,1)S(1)} collective-permute-done((bf16[48,1024]{1,0:T(8,128)(2,1)S(1)}, bf16[48,1024]{1,0:T(8,128)(2,1)S(1)}, u32[]{:S(2)}, u32[]{:S(2)}) %collective-permute-start.58) | collective-permute-done | bytes 98336 | tf_op jit(solution)/shard_map/ppermute | solution.py:25
  129.8 2.5 %collective-permute-done.55.refs_3_ = bf16[48,1024]{1,0:T(8,128)(2,1)S(1)} collective-permute-done((bf16[48,1024]{1,0:T(8,128)(2,1)S(1)}, bf16[48,1024]{1,0:T(8,128)(2,1)S(1)}, u32[]{:S(2)}, u32[]{:S(2)}) %collective-permute-start.55) | collective-permute-done | bytes 98336 | tf_op jit(solution)/shard_map/ppermute | solution.py:25
  132.3 3.0 %collective-permute-done.56.refs_4_ = bf16[48,1024]{1,0:T(8,128)(2,1)S(1)} collective-permute-done((bf16[48,1024]{1,0:T(8,128)(2,1)S(1)}, bf16[48,1024]{1,0:T(8,128)(2,1)S(1)}, u32[]{:S(2)}, u32[]{:S(2)}) %collective-permute-start.56) | collective-permute-done | bytes 98336 | tf_op jit(solution)/shard_map/ppermute | solution.py:25
  (148 shorter events, 52.1 us)
Async XLA Ops:
  9.1 21.7 %collective-permute-start = (bf16[128,1024]{1,0:T(8,128)(2,1)S(1)}, bf16[128,1024]{1,0:T(8,128)(2,1)S(1)}, u32[]{:S(2)}, u32[]{:S(2)}) collective-permute-start(bf16[128,1024]{1,0:T(8,128)(2,1)S(1)} %fusion.2.refs_0_), channel_id=1, source_target_pairs={{0,8},{8,0},{16,24},{24,16},{1,9},{9,1},{17,25},{25,17},{2,10},{10... | collective-permute-start | bytes 786440 | tf_op jit(solution)/shard_map/ppermute | solution.py:25
  9.1 10.4 %collective-permute-start.6 = (bf16[128,384]{1,0:T(8,128)(2,1)S(1)}, bf16[128,384]{1,0:T(8,128)(2,1)S(1)}, u32[]{:S(2)}, u32[]{:S(2)}) collective-permute-start(bf16[128,384]{1,0:T(8,128)(2,1)S(1)} %pad_maximum_fusion.refs_4_), channel_id=1, source_target_pairs={{0,4},{1,5},{2,6},{3,7},{4,0},{5,1},{6,2},{7,3},{8,12},{9,13},{10,... | collective-permute-start | bytes 294920 | tf_op jit(solution)/shard_map/ppermute | solution.py:25
  11.7 9.4 %collective-permute-start.8 = (bf16[128,384]{1,0:T(8,128)(2,1)S(1)}, bf16[128,384]{1,0:T(8,128)(2,1)S(1)}, u32[]{:S(2)}, u32[]{:S(2)}) collective-permute-start(bf16[128,384]{1,0:T(8,128)(2,1)S(1)} %pad_maximum_fusion.refs_4_), channel_id=1, source_target_pairs={{0,6},{1,7},{2,4},{3,5},{4,2},{5,3},{6,0},{7,1},{8,14},{9,15},{10,... | collective-permute-start | bytes 294920 | tf_op jit(solution)/shard_map/ppermute | solution.py:25
  12.2 9.4 %collective-permute-start.3 = (bf16[128,384]{1,0:T(8,128)(2,1)S(1)}, bf16[128,384]{1,0:T(8,128)(2,1)S(1)}, u32[]{:S(2)}, u32[]{:S(2)}) collective-permute-start(bf16[128,384]{1,0:T(8,128)(2,1)S(1)} %pad_maximum_fusion.refs_4_), channel_id=1, source_target_pairs={{0,1},{1,0},{2,3},{3,2},{4,5},{5,4},{6,7},{7,6},{8,9},{9,8},{10,11... | collective-permute-start | bytes 294920 | tf_op jit(solution)/shard_map/ppermute | solution.py:25
  13.9 18.4 %collective-permute-start.2 = (bf16[128,1024]{1,0:T(8,128)(2,1)S(1)}, bf16[128,1024]{1,0:T(8,128)(2,1)S(1)}, u32[]{:S(2)}, u32[]{:S(2)}) collective-permute-start(bf16[128,1024]{1,0:T(8,128)(2,1)S(1)} %collective-permute-done.1.refs_2_), channel_id=1, source_target_pairs={{0,8},{8,0},{16,24},{24,16},{1,9},{9,1},{17,25},{25,17},{2,10},{10... | collective-permute-start | bytes 786440 | tf_op jit(solution)/shard_map/ppermute | solution.py:25
  27.3 10.9 %collective-permute-start.17 = (bf16[128,512]{1,0:T(8,128)(2,1)S(1)}, bf16[128,512]{1,0:T(8,128)(2,1)S(1)}, u32[]{:S(2)}, u32[]{:S(2)}) collective-permute-start(bf16[128,512]{1,0:T(8,128)(2,1)S(1)} %constant_dynamic-slice_fusion.refs_4_), channel_id=1, source_target_pairs={{0,4},{1,5},{2,6},{3,7},{4,0},{5,1},{6,2},{7,3},{8,12},{9,13},{10,... | collective-permute-start | bytes 393224 | tf_op jit(solution)/shard_map/ppermute | solution.py:25
  28.9 10.8 %collective-permute-start.19 = (bf16[128,512]{1,0:T(8,128)(2,1)S(1)}, bf16[128,512]{1,0:T(8,128)(2,1)S(1)}, u32[]{:S(2)}, u32[]{:S(2)}) collective-permute-start(bf16[128,512]{1,0:T(8,128)(2,1)S(1)} %constant_dynamic-slice_fusion.refs_4_), channel_id=1, source_target_pairs={{0,6},{1,7},{2,4},{3,5},{4,2},{5,3},{6,0},{7,1},{8,14},{9,15},{10,... | collective-permute-start | bytes 393224 | tf_op jit(solution)/shard_map/ppermute | solution.py:25
  30.8 9.4 %collective-permute-start.14 = (bf16[128,512]{1,0:T(8,128)(2,1)S(1)}, bf16[128,512]{1,0:T(8,128)(2,1)S(1)}, u32[]{:S(2)}, u32[]{:S(2)}) collective-permute-start(bf16[128,512]{1,0:T(8,128)(2,1)S(1)} %constant_dynamic-slice_fusion.refs_4_), channel_id=1, source_target_pairs={{0,1},{1,0},{2,3},{3,2},{4,5},{5,4},{6,7},{7,6},{8,9},{9,8},{10,11... | collective-permute-start | bytes 393224 | tf_op jit(solution)/shard_map/ppermute | solution.py:25
  33.8 9.6 %collective-permute-start.21 = (bf16[128,512]{1,0:T(8,128)(2,1)S(1)}, bf16[128,512]{1,0:T(8,128)(2,1)S(1)}, u32[]{:S(2)}, u32[]{:S(2)}) collective-permute-start(bf16[128,512]{1,0:T(8,128)(2,1)S(1)} %constant_dynamic-slice_fusion.refs_4_), channel_id=1, source_target_pairs={{0,8},{8,0},{16,24},{24,16},{1,9},{9,1},{17,25},{25,17},{2,10},{10... | collective-permute-start | bytes 393224 | tf_op jit(solution)/shard_map/ppermute | solution.py:25
  53.5 14.3 %collective-permute-start.30 = (bf16[48,1024]{1,0:T(8,128)(2,1)S(1)}, bf16[48,1024]{1,0:T(8,128)(2,1)S(1)}, u32[]{:S(2)}, u32[]{:S(2)}) collective-permute-start(bf16[48,1024]{1,0:T(8,128)(2,1)S(1)} %get-tuple-element.63), channel_id=1, source_target_pairs={{0,4},{1,5},{2,6},{3,7},{4,0},{5,1},{6,2},{7,3},{8,12},{9,13},{10,... | collective-permute-start | bytes 294920 | tf_op jit(solution)/shard_map/ppermute | solution.py:25
  55.1 15.6 %collective-permute-start.31 = (bf16[48,1024]{1,0:T(8,128)(2,1)S(1)}, bf16[48,1024]{1,0:T(8,128)(2,1)S(1)}, u32[]{:S(2)}, u32[]{:S(2)}) collective-permute-start(bf16[48,1024]{1,0:T(8,128)(2,1)S(1)} %get-tuple-element.64), channel_id=1, source_target_pairs={{0,5},{1,4},{2,7},{3,6},{4,1},{5,0},{6,3},{7,2},{8,13},{9,12},{10,... | collective-permute-start | bytes 294920 | tf_op jit(solution)/shard_map/ppermute | solution.py:25
  56.5 14.9 %collective-permute-start.32 = (bf16[48,1024]{1,0:T(8,128)(2,1)S(1)}, bf16[48,1024]{1,0:T(8,128)(2,1)S(1)}, u32[]{:S(2)}, u32[]{:S(2)}) collective-permute-start(bf16[48,1024]{1,0:T(8,128)(2,1)S(1)} %get-tuple-element.66), channel_id=1, source_target_pairs={{0,7},{1,6},{2,5},{3,4},{4,3},{5,2},{6,1},{7,0},{8,15},{9,14},{10,... | collective-permute-start | bytes 294920 | tf_op jit(solution)/shard_map/ppermute | solution.py:25
  59.5 12.5 %collective-permute-start.29 = (bf16[48,1024]{1,0:T(8,128)(2,1)S(1)}, bf16[48,1024]{1,0:T(8,128)(2,1)S(1)}, u32[]{:S(2)}, u32[]{:S(2)}) collective-permute-start(bf16[48,1024]{1,0:T(8,128)(2,1)S(1)} %get-tuple-element.62), channel_id=1, source_target_pairs={{0,6},{1,7},{2,4},{3,5},{4,2},{5,3},{6,0},{7,1},{8,14},{9,15},{10,... | collective-permute-start | bytes 294920 | tf_op jit(solution)/shard_map/ppermute | solution.py:25
  61.3 10.8 %collective-permute-start.35 = (bf16[48,1024]{1,0:T(8,128)(2,1)S(1)}, bf16[48,1024]{1,0:T(8,128)(2,1)S(1)}, u32[]{:S(2)}, u32[]{:S(2)}) collective-permute-start(bf16[48,1024]{1,0:T(8,128)(2,1)S(1)} %get-tuple-element.73), channel_id=1, source_target_pairs={{0,3},{1,2},{2,1},{3,0},{4,7},{5,6},{6,5},{7,4},{8,11},{9,10},{10,... | collective-permute-start | bytes 294920 | tf_op jit(solution)/shard_map/ppermute | solution.py:25
  72.1 13.6 %collective-permute-start.40 = (bf16[96,1024]{1,0:T(8,128)(2,1)S(1)}, bf16[96,1024]{1,0:T(8,128)(2,1)S(1)}, u32[]{:S(2)}, u32[]{:S(2)}) collective-permute-start(bf16[96,1024]{1,0:T(8,128)(2,1)S(1)} %constant_dynamic-update-slice_fusion.2.refs_0_), channel_id=1, source_target_pairs={{0,16},{8,24},{16,0},{24,8},{1,17},{9,25},{17,1},{25,9},{2,18},{10... | collective-permute-start | bytes 589832 | tf_op jit(solution)/shard_map/ppermute | solution.py:25
  79.3 12.0 %collective-permute-start.37 = (bf16[192,1024]{1,0:T(8,128)(2,1)S(1)}, bf16[192,1024]{1,0:T(8,128)(2,1)S(1)}, u32[]{:S(2)}, u32[]{:S(2)}) collective-permute-start(bf16[192,1024]{1,0:T(8,128)(2,1)S(1)} %constant_dynamic-update-slice_fusion.4.refs_0_), channel_id=1, source_target_pairs={{0,16},{8,24},{16,0},{24,8},{1,17},{9,25},{17,1},{25,9},{2,18},{10... | collective-permute-start | bytes 1179656 | tf_op jit(solution)/shard_map/ppermute | solution.py:25
  86.5 11.1 %collective-permute-start.38 = (bf16[192,1024]{1,0:T(8,128)(2,1)S(1)}, bf16[192,1024]{1,0:T(8,128)(2,1)S(1)}, u32[]{:S(2)}, u32[]{:S(2)}) collective-permute-start(bf16[192,1024]{1,0:T(8,128)(2,1)S(1)} %constant_dynamic-update-slice_fusion.4.refs_0_), channel_id=1, source_target_pairs={{0,8},{8,0},{16,24},{24,16},{1,9},{9,1},{17,25},{25,17},{2,10},{10... | collective-permute-start | bytes 1179656 | tf_op jit(solution)/shard_map/ppermute | solution.py:25
  86.7 9.4 %collective-permute-start.49 = (bf16[96,1024]{1,0:T(8,128)(2,1)S(1)}, bf16[96,1024]{1,0:T(8,128)(2,1)S(1)}, u32[]{:S(2)}, u32[]{:S(2)}) collective-permute-start(bf16[96,1024]{1,0:T(8,128)(2,1)S(1)} %shard_map.126), channel_id=1, source_target_pairs={{0,16},{8,24},{16,0},{24,8},{1,17},{9,25},{17,1},{25,9},{2,18},{10... | collective-permute-start | bytes 589832 | tf_op jit(solution)/shard_map/ppermute | solution.py:25
  105.9 12.6 %collective-permute-start.50 = (bf16[192,1024]{1,0:T(8,128)(2,1)S(1)}, bf16[192,1024]{1,0:T(8,128)(2,1)S(1)}, u32[]{:S(2)}, u32[]{:S(2)}) collective-permute-start(bf16[192,1024]{1,0:T(8,128)(2,1)S(1)} %get-tuple-element.95), channel_id=1, source_target_pairs={{0,8},{8,0},{16,24},{24,16},{1,9},{9,1},{17,25},{25,17},{2,10},{10... | collective-permute-start | bytes 1179656 | tf_op jit(solution)/shard_map/ppermute | solution.py:25
  112.5 10.4 %collective-permute-start.53 = (bf16[192,1024]{1,0:T(8,128)(2,1)S(1)}, bf16[192,1024]{1,0:T(8,128)(2,1)S(1)}, u32[]{:S(2)}, u32[]{:S(2)}) collective-permute-start(bf16[192,1024]{1,0:T(8,128)(2,1)S(1)} %shard_map.134), channel_id=1, source_target_pairs={{0,16},{8,24},{16,0},{24,8},{1,17},{9,25},{17,1},{25,9},{2,18},{10... | collective-permute-start | bytes 1179656 | tf_op jit(solution)/shard_map/ppermute | solution.py:25
  113.0 14.0 %collective-permute-start.57 = (bf16[48,1024]{1,0:T(8,128)(2,1)S(1)}, bf16[48,1024]{1,0:T(8,128)(2,1)S(1)}, u32[]{:S(2)}, u32[]{:S(2)}) collective-permute-start(bf16[48,1024]{1,0:T(8,128)(2,1)S(1)} %get-tuple-element.88), channel_id=1, source_target_pairs={{0,4},{1,5},{2,6},{3,7},{4,0},{5,1},{6,2},{7,3},{8,12},{9,13},{10,... | collective-permute-start | bytes 294920 | tf_op jit(solution)/shard_map/ppermute | solution.py:25
  115.0 14.8 %collective-permute-start.58 = (bf16[48,1024]{1,0:T(8,128)(2,1)S(1)}, bf16[48,1024]{1,0:T(8,128)(2,1)S(1)}, u32[]{:S(2)}, u32[]{:S(2)}) collective-permute-start(bf16[48,1024]{1,0:T(8,128)(2,1)S(1)} %get-tuple-element.89), channel_id=1, source_target_pairs={{0,5},{1,4},{2,7},{3,6},{4,1},{5,0},{6,3},{7,2},{8,13},{9,12},{10,... | collective-permute-start | bytes 294920 | tf_op jit(solution)/shard_map/ppermute | solution.py:25
  116.3 13.5 %collective-permute-start.59 = (bf16[48,1024]{1,0:T(8,128)(2,1)S(1)}, bf16[48,1024]{1,0:T(8,128)(2,1)S(1)}, u32[]{:S(2)}, u32[]{:S(2)}) collective-permute-start(bf16[48,1024]{1,0:T(8,128)(2,1)S(1)} %get-tuple-element.104), channel_id=1, source_target_pairs={{0,6},{1,7},{2,4},{3,5},{4,2},{5,3},{6,0},{7,1},{8,14},{9,15},{10,... | collective-permute-start | bytes 294920 | tf_op jit(solution)/shard_map/ppermute | solution.py:25
  118.6 11.2 %collective-permute-start.60 = (bf16[48,1024]{1,0:T(8,128)(2,1)S(1)}, bf16[48,1024]{1,0:T(8,128)(2,1)S(1)}, u32[]{:S(2)}, u32[]{:S(2)}) collective-permute-start(bf16[48,1024]{1,0:T(8,128)(2,1)S(1)} %get-tuple-element.105), channel_id=1, source_target_pairs={{0,7},{1,6},{2,5},{3,4},{4,3},{5,2},{6,1},{7,0},{8,15},{9,14},{10,... | collective-permute-start | bytes 294920 | tf_op jit(solution)/shard_map/ppermute | solution.py:25
  (44 other events, 438.5 us)

commit v4 on v3

--- a/solution.py
+++ b/solution.py
@@ -326,7 +326,7 @@
     )
     attention_out, route, buffers = results[0], results[1], results[2:]
 
-    groups = ((4, 5), (6, 7), (0, 1, 2, 3)) if small else ((0,),)
+    groups = ((6, 7), (4, 5), (0, 1, 2, 3)) if small else ((0,),)
     received = {}
     if small:
         received[0] = buffers[0]

time: 137 us -> 136 us (level)
  waiting for transfers between devices: 60.3 us -> 48.4 us
  starting transfers between devices: 47.9 us -> 59.3 us
    ppermute x61, waiting for transfers between devices: 60.3 us -> 48.4 us  [swap(): return lax.ppermute(value, axis, [(i, i ^ bits) for i in range(size)])]
    ppermute x61, starting transfers between devices: 47.9 us -> 59.3 us  [swap(): return lax.ppermute(value, axis, [(i, i ^ bits) for i in range(size)])]
  transfers between devices with their start and end apart: 61 -> 61, of which waited for: 30 -> 27; matrix products, arithmetic and copies ran while one was open for 0% -> 0% of each run, Pallas kernels for 9% -> 9%
where the time goes in v4:
time: 136 us
  starting transfers between devices  59.3 us (44%)
  waiting for transfers between devices  48.4 us (36%)
  Pallas kernels  23 us (17%)
  other arithmetic  2.26 us (2%)
  local copies, waits for them, and re-layouts  2.06 us (2%)
    ppermute x61, starting transfers between devices, swap(): return lax.ppermute(value, axis, [(i, i ^ bits) for i in range(size)])  59.3 us
    ppermute x61, waiting for transfers between devices, swap(): return lax.ppermute(value, axis, [(i, i ^ bits) for i in range(size)])  48.4 us
    pallas_call x16, Pallas kernels, call(): pl.pallas_call(kernel, out_shape=outs, in_specs=[SMEM] + [VMEM] * (len(ar...  23 us
  transfers between devices with their start and end apart: 61, of which 27 were waited for; matrix products, arithmetic and copies ran while one was open for 0% of the time, Pallas kernels for 9%

profile of v4, /device:TPU:0, one launch (start us, length us, event | category | flops | bytes accessed | tf_op | source)
XLA Modules:
  0.0 136.0 jit_solution(11574911935986362688)
XLA Ops:
  4.6 3.0 %collective-permute-start.1 = (bf16[128,1024]{1,0:T(8,128)(2,1)S(1)}, bf16[128,1024]{1,0:T(8,128)(2,1)S(1)}, u32[]{:S(2)}, u32[]{:S(2)}) collective-permute-start(bf16[128,1024]{1,0:T(8,128)(2,1)S(1)} %fusion.2.refs_0_), channel_id=1, source_target_pairs={{0,16},{8,24},{16,0},{24,8},{1,17},{9,25},{17,1},{25,9},{2,18},{10... | collective-permute-start | bytes 786440 | tf_op jit(solution)/shard_map/ppermute | solution.py:25
  9.1 2.6 %collective-permute-start.6 = (bf16[128,384]{1,0:T(8,128)(2,1)S(1)}, bf16[128,384]{1,0:T(8,128)(2,1)S(1)}, u32[]{:S(2)}, u32[]{:S(2)}) collective-permute-start(bf16[128,384]{1,0:T(8,128)(2,1)S(1)} %pad_maximum_fusion.refs_4_), channel_id=1, source_target_pairs={{0,4},{1,5},{2,6},{3,7},{4,0},{5,1},{6,2},{7,3},{8,12},{9,13},{10,... | collective-permute-start | bytes 294920 | tf_op jit(solution)/shard_map/ppermute | solution.py:25
  13.9 5.7 %collective-permute-done.6.refs_8_ = bf16[128,384]{1,0:T(8,128)(2,1)S(1)} collective-permute-done((bf16[128,384]{1,0:T(8,128)(2,1)S(1)}, bf16[128,384]{1,0:T(8,128)(2,1)S(1)}, u32[]{:S(2)}, u32[]{:S(2)}) %collective-permute-start.6) | collective-permute-done | bytes 98336 | tf_op jit(solution)/shard_map/ppermute | solution.py:25
  23.1 2.1 %collective-permute-done.5.refs_7_ = bf16[128,384]{1,0:T(8,128)(2,1)S(1)} collective-permute-done((bf16[128,384]{1,0:T(8,128)(2,1)S(1)}, bf16[128,384]{1,0:T(8,128)(2,1)S(1)}, u32[]{:S(2)}, u32[]{:S(2)}) %collective-permute-start.5) | collective-permute-done | bytes 98336 | tf_op jit(solution)/shard_map/ppermute | solution.py:25
  25.2 2.0 %collective-permute-done.7.refs_9_ = bf16[128,384]{1,0:T(8,128)(2,1)S(1)} collective-permute-done((bf16[128,384]{1,0:T(8,128)(2,1)S(1)}, bf16[128,384]{1,0:T(8,128)(2,1)S(1)}, u32[]{:S(2)}, u32[]{:S(2)}) %collective-permute-start.7) | collective-permute-done | bytes 98336 | tf_op jit(solution)/shard_map/ppermute | solution.py:25
  28.9 1.9 %collective-permute-start.19 = (bf16[128,512]{1,0:T(8,128)(2,1)S(1)}, bf16[128,512]{1,0:T(8,128)(2,1)S(1)}, u32[]{:S(2)}, u32[]{:S(2)}) collective-permute-start(bf16[128,512]{1,0:T(8,128)(2,1)S(1)} %constant_dynamic-slice_fusion.refs_4_), channel_id=1, source_target_pairs={{0,6},{1,7},{2,4},{3,5},{4,2},{5,3},{6,0},{7,1},{8,14},{9,15},{10,... | collective-permute-start | bytes 393224 | tf_op jit(solution)/shard_map/ppermute | solution.py:25
  34.3 3.9 %collective-permute-done.17.refs_8_ = bf16[128,512]{1,0:T(8,128)(2,1)S(1)} collective-permute-done((bf16[128,512]{1,0:T(8,128)(2,1)S(1)}, bf16[128,512]{1,0:T(8,128)(2,1)S(1)}, u32[]{:S(2)}, u32[]{:S(2)}) %collective-permute-start.17) | collective-permute-done | bytes 131104 | tf_op jit(solution)/shard_map/ppermute | solution.py:25
  46.8 2.7 %collective-permute-done.12 = bf16[256,256]{1,0:T(8,128)(2,1)S(1)} collective-permute-done((bf16[256,256]{1,0:T(8,128)(2,1)S(1)}, bf16[256,256]{1,0:T(8,128)(2,1)S(1)}, u32[]{:S(2)}, u32[]{:S(2)}) %collective-permute-start.12) | collective-permute-done | bytes 131104 | tf_op jit(solution)/shard_map/ppermute | solution.py:25
  51.3 2.2 %shard_map.124 = (bf16[128,1024]{1,0:T(8,128)(2,1)}, f32[128,128]{1,0:T(8,128)S(1)}, bf16[48,1024]{1,0:T(8,128)(2,1)S(1)}, bf16[48,1024]{1,0:T(8,128)(2,1)S(1)},...) custom-call(s32[3]{0:T(128)S(1)} %pad_add_fusion.place, ...), custom_call_target="tpu_custom_call" | custom-call | flops 369098752 | bytes 3757068 | tf_op jit(solution)/shard_map/pallas_call | solution.py:32
  53.5 2.1 %collective-permute-start.30 = (bf16[48,1024]{1,0:T(8,128)(2,1)S(1)}, bf16[48,1024]{1,0:T(8,128)(2,1)S(1)}, u32[]{:S(2)}, u32[]{:S(2)}) collective-permute-start(bf16[48,1024]{1,0:T(8,128)(2,1)S(1)} %get-tuple-element.63), channel_id=1, source_target_pairs={{0,6},{1,7},{2,4},{3,5},{4,2},{5,3},{6,0},{7,1},{8,14},{9,15},{10,... | collective-permute-start | bytes 294920 | tf_op jit(solution)/shard_map/ppermute | solution.py:25
  58.0 3.2 %collective-permute-start.29 = (bf16[48,1024]{1,0:T(8,128)(2,1)S(1)}, bf16[48,1024]{1,0:T(8,128)(2,1)S(1)}, u32[]{:S(2)}, u32[]{:S(2)}) collective-permute-start(bf16[48,1024]{1,0:T(8,128)(2,1)S(1)} %get-tuple-element.62), channel_id=1, source_target_pairs={{0,4},{1,5},{2,6},{3,7},{4,0},{5,1},{6,2},{7,3},{8,12},{9,13},{10,... | collective-permute-start | bytes 294920 | tf_op jit(solution)/shard_map/ppermute | solution.py:25
  61.4 5.8 %collective-permute-start.34 = (bf16[48,1024]{1,0:T(8,128)(2,1)S(1)}, bf16[48,1024]{1,0:T(8,128)(2,1)S(1)}, u32[]{:S(2)}, u32[]{:S(2)}) collective-permute-start(bf16[48,1024]{1,0:T(8,128)(2,1)S(1)} %get-tuple-element.71), channel_id=1, source_target_pairs={{0,2},{1,3},{2,0},{3,1},{4,6},{5,7},{6,4},{7,5},{8,10},{9,11},{10,... | collective-permute-start | bytes 294920 | tf_op jit(solution)/shard_map/ppermute | solution.py:25
  67.1 2.6 %collective-permute-start.33 = (bf16[48,1024]{1,0:T(8,128)(2,1)S(1)}, bf16[48,1024]{1,0:T(8,128)(2,1)S(1)}, u32[]{:S(2)}, u32[]{:S(2)}) collective-permute-start(bf16[48,1024]{1,0:T(8,128)(2,1)S(1)} %get-tuple-element.69), channel_id=1, source_target_pairs={{0,1},{1,0},{2,3},{3,2},{4,5},{5,4},{6,7},{7,6},{8,9},{9,8},{10,11... | collective-permute-start | bytes 294920 | tf_op jit(solution)/shard_map/ppermute | solution.py:25
  69.7 3.1 %collective-permute-done.32 = bf16[48,1024]{1,0:T(8,128)(2,1)S(1)} collective-permute-done((bf16[48,1024]{1,0:T(8,128)(2,1)S(1)}, bf16[48,1024]{1,0:T(8,128)(2,1)S(1)}, u32[]{:S(2)}, u32[]{:S(2)}) %collective-permute-start.32) | collective-permute-done | bytes 98336 | tf_op jit(solution)/shard_map/ppermute | solution.py:25
  75.0 5.4 %collective-permute-done.36.refs_1_ = bf16[96,1024]{1,0:T(8,128)(2,1)S(1)} collective-permute-done((bf16[96,1024]{1,0:T(8,128)(2,1)S(1)}, bf16[96,1024]{1,0:T(8,128)(2,1)S(1)}, u32[]{:S(2)}, u32[]{:S(2)}) %collective-permute-start.36) | collective-permute-done | bytes 196640 | tf_op jit(solution)/shard_map/ppermute | solution.py:25
  81.8 4.2 %shard_map.125 = (bf16[96,1024]{1,0:T(8,128)(2,1)S(1)}, bf16[96,1024]{1,0:T(8,128)(2,1)S(1)}, bf16[96,1024]{1,0:T(8,128)(2,1)S(1)}, bf16[96,1024]{1,0:T(8,128)(2,1)S(1)}) custom-call(bf16[96,1024]{1,0:T(8,128)(2,1)S(1)} %constant_dynamic-update-slice_fusion.refs_0_, bf16[96,1024]{1,0:T(8,128)(2,1)S(1)} %collective-permute-done.36.refs_1_, ...), custom_call_target="tpu_custom_call" | custom-call | flops 2415919104 | bytes 7864320 | tf_op jit(solution)/shard_map/pallas_call | solution.py:32
  88.7 3.7 %collective-permute-done.37.refs_1_ = bf16[192,1024]{1,0:T(8,128)(2,1)S(1)} collective-permute-done((bf16[192,1024]{1,0:T(8,128)(2,1)S(1)}, bf16[192,1024]{1,0:T(8,128)(2,1)S(1)}, u32[]{:S(2)}, u32[]{:S(2)}) %collective-permute-start.37) | collective-permute-done | bytes 393248 | tf_op jit(solution)/shard_map/ppermute | solution.py:25
  92.4 4.2 %shard_map.128 = (bf16[96,1024]{1,0:T(8,128)(2,1)S(1)}, bf16[96,1024]{1,0:T(8,128)(2,1)S(1)}, bf16[96,1024]{1,0:T(8,128)(2,1)S(1)}, bf16[96,1024]{1,0:T(8,128)(2,1)S(1)}) custom-call(bf16[96,1024]{1,0:T(8,128)(2,1)S(1)} %constant_dynamic-update-slice_fusion.2.refs_0_, bf16[96,1024]{1,0:T(8,128)(2,1)S(1)} %collective-permute-done.40.refs_1_, ...), custom_call_target="tpu_custom_call" | custom-call | flops 2415919104 | bytes 7864320 | tf_op jit(solution)/shard_map/pallas_call | solution.py:32
  98.7 7.5 %shard_map.132 = (bf16[192,1024]{1,0:T(8,128)(2,1)S(1)}, bf16[192,1024]{1,0:T(8,128)(2,1)S(1)}, bf16[192,1024]{1,0:T(8,128)(2,1)S(1)}, bf16[192,1024]{1,0:T(8,128)(2,1)S(1)}) custom-call(bf16[192,1024]{1,0:T(8,128)(2,1)S(1)} %constant_dynamic-update-slice_fusion.4.refs_0_, bf16[192,1024]{1,0:T(8,128)(2,1)S(1)} %collective-permute-done.37.refs_1_, ...), custom_call_target="tpu_custom_call" | custom-call | flops 4831838208 | bytes 9437184 | tf_op jit(solution)/shard_map/pallas_call | solution.py:32
  108.1 5.5 %collective-permute-done.52.refs_1_ = bf16[96,1024]{1,0:T(8,128)(2,1)S(1)} collective-permute-done((bf16[96,1024]{1,0:T(8,128)(2,1)S(1)}, bf16[96,1024]{1,0:T(8,128)(2,1)S(1)}, u32[]{:S(2)}, u32[]{:S(2)}) %collective-permute-start.52) | collective-permute-done | bytes 196640 | tf_op jit(solution)/shard_map/ppermute | solution.py:25
  113.8 1.9 %collective-permute-start.59 = (bf16[48,1024]{1,0:T(8,128)(2,1)S(1)}, bf16[48,1024]{1,0:T(8,128)(2,1)S(1)}, u32[]{:S(2)}, u32[]{:S(2)}) collective-permute-start(bf16[48,1024]{1,0:T(8,128)(2,1)S(1)} %get-tuple-element.88), channel_id=1, source_target_pairs={{0,6},{1,7},{2,4},{3,5},{4,2},{5,3},{6,0},{7,1},{8,14},{9,15},{10,... | collective-permute-start | bytes 294920 | tf_op jit(solution)/shard_map/ppermute | solution.py:25
  117.9 3.8 %collective-permute-start.58 = (bf16[48,1024]{1,0:T(8,128)(2,1)S(1)}, bf16[48,1024]{1,0:T(8,128)(2,1)S(1)}, u32[]{:S(2)}, u32[]{:S(2)}) collective-permute-start(bf16[48,1024]{1,0:T(8,128)(2,1)S(1)} %get-tuple-element.105), channel_id=1, source_target_pairs={{0,5},{1,4},{2,7},{3,6},{4,1},{5,0},{6,3},{7,2},{8,13},{9,12},{10,... | collective-permute-start | bytes 294920 | tf_op jit(solution)/shard_map/ppermute | solution.py:25
  121.7 2.3 %collective-permute-done.53.refs_1_ = bf16[192,1024]{1,0:T(8,128)(2,1)S(1)} collective-permute-done((bf16[192,1024]{1,0:T(8,128)(2,1)S(1)}, bf16[192,1024]{1,0:T(8,128)(2,1)S(1)}, u32[]{:S(2)}, u32[]{:S(2)}) %collective-permute-start.53) | collective-permute-done | bytes 393248 | tf_op jit(solution)/shard_map/ppermute | solution.py:25
  124.6 5.5 %collective-permute-start.56 = (bf16[48,1024]{1,0:T(8,128)(2,1)S(1)}, bf16[48,1024]{1,0:T(8,128)(2,1)S(1)}, u32[]{:S(2)}, u32[]{:S(2)}) collective-permute-start(bf16[48,1024]{1,0:T(8,128)(2,1)S(1)} %get-tuple-element.103), channel_id=1, source_target_pairs={{0,3},{1,2},{2,1},{3,0},{4,7},{5,6},{6,5},{7,4},{8,11},{9,10},{10,... | collective-permute-start | bytes 294920 | tf_op jit(solution)/shard_map/ppermute | solution.py:25
  (148 shorter events, 48.0 us)
Async XLA Ops:
  9.1 21.7 %collective-permute-start = (bf16[128,1024]{1,0:T(8,128)(2,1)S(1)}, bf16[128,1024]{1,0:T(8,128)(2,1)S(1)}, u32[]{:S(2)}, u32[]{:S(2)}) collective-permute-start(bf16[128,1024]{1,0:T(8,128)(2,1)S(1)} %fusion.2.refs_0_), channel_id=1, source_target_pairs={{0,8},{8,0},{16,24},{24,16},{1,9},{9,1},{17,25},{25,17},{2,10},{10... | collective-permute-start | bytes 786440 | tf_op jit(solution)/shard_map/ppermute | solution.py:25
  9.1 10.4 %collective-permute-start.6 = (bf16[128,384]{1,0:T(8,128)(2,1)S(1)}, bf16[128,384]{1,0:T(8,128)(2,1)S(1)}, u32[]{:S(2)}, u32[]{:S(2)}) collective-permute-start(bf16[128,384]{1,0:T(8,128)(2,1)S(1)} %pad_maximum_fusion.refs_4_), channel_id=1, source_target_pairs={{0,4},{1,5},{2,6},{3,7},{4,0},{5,1},{6,2},{7,3},{8,12},{9,13},{10,... | collective-permute-start | bytes 294920 | tf_op jit(solution)/shard_map/ppermute | solution.py:25
  11.7 9.4 %collective-permute-start.8 = (bf16[128,384]{1,0:T(8,128)(2,1)S(1)}, bf16[128,384]{1,0:T(8,128)(2,1)S(1)}, u32[]{:S(2)}, u32[]{:S(2)}) collective-permute-start(bf16[128,384]{1,0:T(8,128)(2,1)S(1)} %pad_maximum_fusion.refs_4_), channel_id=1, source_target_pairs={{0,6},{1,7},{2,4},{3,5},{4,2},{5,3},{6,0},{7,1},{8,14},{9,15},{10,... | collective-permute-start | bytes 294920 | tf_op jit(solution)/shard_map/ppermute | solution.py:25
  12.2 9.4 %collective-permute-start.3 = (bf16[128,384]{1,0:T(8,128)(2,1)S(1)}, bf16[128,384]{1,0:T(8,128)(2,1)S(1)}, u32[]{:S(2)}, u32[]{:S(2)}) collective-permute-start(bf16[128,384]{1,0:T(8,128)(2,1)S(1)} %pad_maximum_fusion.refs_4_), channel_id=1, source_target_pairs={{0,1},{1,0},{2,3},{3,2},{4,5},{5,4},{6,7},{7,6},{8,9},{9,8},{10,11... | collective-permute-start | bytes 294920 | tf_op jit(solution)/shard_map/ppermute | solution.py:25
  13.9 18.4 %collective-permute-start.2 = (bf16[128,1024]{1,0:T(8,128)(2,1)S(1)}, bf16[128,1024]{1,0:T(8,128)(2,1)S(1)}, u32[]{:S(2)}, u32[]{:S(2)}) collective-permute-start(bf16[128,1024]{1,0:T(8,128)(2,1)S(1)} %collective-permute-done.1.refs_2_), channel_id=1, source_target_pairs={{0,8},{8,0},{16,24},{24,16},{1,9},{9,1},{17,25},{25,17},{2,10},{10... | collective-permute-start | bytes 786440 | tf_op jit(solution)/shard_map/ppermute | solution.py:25
  27.3 10.9 %collective-permute-start.17 = (bf16[128,512]{1,0:T(8,128)(2,1)S(1)}, bf16[128,512]{1,0:T(8,128)(2,1)S(1)}, u32[]{:S(2)}, u32[]{:S(2)}) collective-permute-start(bf16[128,512]{1,0:T(8,128)(2,1)S(1)} %constant_dynamic-slice_fusion.refs_4_), channel_id=1, source_target_pairs={{0,4},{1,5},{2,6},{3,7},{4,0},{5,1},{6,2},{7,3},{8,12},{9,13},{10,... | collective-permute-start | bytes 393224 | tf_op jit(solution)/shard_map/ppermute | solution.py:25
  28.9 10.8 %collective-permute-start.19 = (bf16[128,512]{1,0:T(8,128)(2,1)S(1)}, bf16[128,512]{1,0:T(8,128)(2,1)S(1)}, u32[]{:S(2)}, u32[]{:S(2)}) collective-permute-start(bf16[128,512]{1,0:T(8,128)(2,1)S(1)} %constant_dynamic-slice_fusion.refs_4_), channel_id=1, source_target_pairs={{0,6},{1,7},{2,4},{3,5},{4,2},{5,3},{6,0},{7,1},{8,14},{9,15},{10,... | collective-permute-start | bytes 393224 | tf_op jit(solution)/shard_map/ppermute | solution.py:25
  30.8 9.4 %collective-permute-start.14 = (bf16[128,512]{1,0:T(8,128)(2,1)S(1)}, bf16[128,512]{1,0:T(8,128)(2,1)S(1)}, u32[]{:S(2)}, u32[]{:S(2)}) collective-permute-start(bf16[128,512]{1,0:T(8,128)(2,1)S(1)} %constant_dynamic-slice_fusion.refs_4_), channel_id=1, source_target_pairs={{0,1},{1,0},{2,3},{3,2},{4,5},{5,4},{6,7},{7,6},{8,9},{9,8},{10,11... | collective-permute-start | bytes 393224 | tf_op jit(solution)/shard_map/ppermute | solution.py:25
  33.8 9.6 %collective-permute-start.21 = (bf16[128,512]{1,0:T(8,128)(2,1)S(1)}, bf16[128,512]{1,0:T(8,128)(2,1)S(1)}, u32[]{:S(2)}, u32[]{:S(2)}) collective-permute-start(bf16[128,512]{1,0:T(8,128)(2,1)S(1)} %constant_dynamic-slice_fusion.refs_4_), channel_id=1, source_target_pairs={{0,8},{8,0},{16,24},{24,16},{1,9},{9,1},{17,25},{25,17},{2,10},{10... | collective-permute-start | bytes 393224 | tf_op jit(solution)/shard_map/ppermute | solution.py:25
  55.7 11.4 %collective-permute-start.31 = (bf16[48,1024]{1,0:T(8,128)(2,1)S(1)}, bf16[48,1024]{1,0:T(8,128)(2,1)S(1)}, u32[]{:S(2)}, u32[]{:S(2)}) collective-permute-start(bf16[48,1024]{1,0:T(8,128)(2,1)S(1)} %get-tuple-element.64), channel_id=1, source_target_pairs={{0,7},{1,6},{2,5},{3,4},{4,3},{5,2},{6,1},{7,0},{8,15},{9,14},{10,... | collective-permute-start | bytes 294920 | tf_op jit(solution)/shard_map/ppermute | solution.py:25
  57.4 15.4 %collective-permute-start.32 = (bf16[48,1024]{1,0:T(8,128)(2,1)S(1)}, bf16[48,1024]{1,0:T(8,128)(2,1)S(1)}, u32[]{:S(2)}, u32[]{:S(2)}) collective-permute-start(bf16[48,1024]{1,0:T(8,128)(2,1)S(1)} %get-tuple-element.66), channel_id=1, source_target_pairs={{0,5},{1,4},{2,7},{3,6},{4,1},{5,0},{6,3},{7,2},{8,13},{9,12},{10,... | collective-permute-start | bytes 294920 | tf_op jit(solution)/shard_map/ppermute | solution.py:25
  58.0 15.4 %collective-permute-start.29 = (bf16[48,1024]{1,0:T(8,128)(2,1)S(1)}, bf16[48,1024]{1,0:T(8,128)(2,1)S(1)}, u32[]{:S(2)}, u32[]{:S(2)}) collective-permute-start(bf16[48,1024]{1,0:T(8,128)(2,1)S(1)} %get-tuple-element.62), channel_id=1, source_target_pairs={{0,4},{1,5},{2,6},{3,7},{4,0},{5,1},{6,2},{7,3},{8,12},{9,13},{10,... | collective-permute-start | bytes 294920 | tf_op jit(solution)/shard_map/ppermute | solution.py:25
  61.3 12.2 %collective-permute-start.35 = (bf16[48,1024]{1,0:T(8,128)(2,1)S(1)}, bf16[48,1024]{1,0:T(8,128)(2,1)S(1)}, u32[]{:S(2)}, u32[]{:S(2)}) collective-permute-start(bf16[48,1024]{1,0:T(8,128)(2,1)S(1)} %get-tuple-element.73), channel_id=1, source_target_pairs={{0,3},{1,2},{2,1},{3,0},{4,7},{5,6},{6,5},{7,4},{8,11},{9,10},{10,... | collective-permute-start | bytes 294920 | tf_op jit(solution)/shard_map/ppermute | solution.py:25
  61.4 13.6 %collective-permute-start.34 = (bf16[48,1024]{1,0:T(8,128)(2,1)S(1)}, bf16[48,1024]{1,0:T(8,128)(2,1)S(1)}, u32[]{:S(2)}, u32[]{:S(2)}) collective-permute-start(bf16[48,1024]{1,0:T(8,128)(2,1)S(1)} %get-tuple-element.71), channel_id=1, source_target_pairs={{0,2},{1,3},{2,0},{3,1},{4,6},{5,7},{6,4},{7,5},{8,10},{9,11},{10,... | collective-permute-start | bytes 294920 | tf_op jit(solution)/shard_map/ppermute | solution.py:25
  73.5 13.3 %collective-permute-start.40 = (bf16[96,1024]{1,0:T(8,128)(2,1)S(1)}, bf16[96,1024]{1,0:T(8,128)(2,1)S(1)}, u32[]{:S(2)}, u32[]{:S(2)}) collective-permute-start(bf16[96,1024]{1,0:T(8,128)(2,1)S(1)} %constant_dynamic-update-slice_fusion.2.refs_0_), channel_id=1, source_target_pairs={{0,16},{8,24},{16,0},{24,8},{1,17},{9,25},{17,1},{25,9},{2,18},{10... | collective-permute-start | bytes 589832 | tf_op jit(solution)/shard_map/ppermute | solution.py:25
  80.4 12.0 %collective-permute-start.37 = (bf16[192,1024]{1,0:T(8,128)(2,1)S(1)}, bf16[192,1024]{1,0:T(8,128)(2,1)S(1)}, u32[]{:S(2)}, u32[]{:S(2)}) collective-permute-start(bf16[192,1024]{1,0:T(8,128)(2,1)S(1)} %constant_dynamic-update-slice_fusion.4.refs_0_), channel_id=1, source_target_pairs={{0,16},{8,24},{16,0},{24,8},{1,17},{9,25},{17,1},{25,9},{2,18},{10... | collective-permute-start | bytes 1179656 | tf_op jit(solution)/shard_map/ppermute | solution.py:25
  87.6 11.1 %collective-permute-start.38 = (bf16[192,1024]{1,0:T(8,128)(2,1)S(1)}, bf16[192,1024]{1,0:T(8,128)(2,1)S(1)}, u32[]{:S(2)}, u32[]{:S(2)}) collective-permute-start(bf16[192,1024]{1,0:T(8,128)(2,1)S(1)} %constant_dynamic-update-slice_fusion.4.refs_0_), channel_id=1, source_target_pairs={{0,8},{8,0},{16,24},{24,16},{1,9},{9,1},{17,25},{25,17},{2,10},{10... | collective-permute-start | bytes 1179656 | tf_op jit(solution)/shard_map/ppermute | solution.py:25
  87.9 9.4 %collective-permute-start.49 = (bf16[96,1024]{1,0:T(8,128)(2,1)S(1)}, bf16[96,1024]{1,0:T(8,128)(2,1)S(1)}, u32[]{:S(2)}, u32[]{:S(2)}) collective-permute-start(bf16[96,1024]{1,0:T(8,128)(2,1)S(1)} %shard_map.126), channel_id=1, source_target_pairs={{0,16},{8,24},{16,0},{24,8},{1,17},{9,25},{17,1},{25,9},{2,18},{10... | collective-permute-start | bytes 589832 | tf_op jit(solution)/shard_map/ppermute | solution.py:25
  106.6 11.2 %collective-permute-start.50 = (bf16[192,1024]{1,0:T(8,128)(2,1)S(1)}, bf16[192,1024]{1,0:T(8,128)(2,1)S(1)}, u32[]{:S(2)}, u32[]{:S(2)}) collective-permute-start(bf16[192,1024]{1,0:T(8,128)(2,1)S(1)} %get-tuple-element.95), channel_id=1, source_target_pairs={{0,8},{8,0},{16,24},{24,16},{1,9},{9,1},{17,25},{25,17},{2,10},{10... | collective-permute-start | bytes 1179656 | tf_op jit(solution)/shard_map/ppermute | solution.py:25
  113.6 10.4 %collective-permute-start.53 = (bf16[192,1024]{1,0:T(8,128)(2,1)S(1)}, bf16[192,1024]{1,0:T(8,128)(2,1)S(1)}, u32[]{:S(2)}, u32[]{:S(2)}) collective-permute-start(bf16[192,1024]{1,0:T(8,128)(2,1)S(1)} %shard_map.134), channel_id=1, source_target_pairs={{0,16},{8,24},{16,0},{24,8},{1,17},{9,25},{17,1},{25,9},{2,18},{10... | collective-permute-start | bytes 1179656 | tf_op jit(solution)/shard_map/ppermute | solution.py:25
  113.8 10.7 %collective-permute-start.59 = (bf16[48,1024]{1,0:T(8,128)(2,1)S(1)}, bf16[48,1024]{1,0:T(8,128)(2,1)S(1)}, u32[]{:S(2)}, u32[]{:S(2)}) collective-permute-start(bf16[48,1024]{1,0:T(8,128)(2,1)S(1)} %get-tuple-element.88), channel_id=1, source_target_pairs={{0,6},{1,7},{2,4},{3,5},{4,2},{5,3},{6,0},{7,1},{8,14},{9,15},{10,... | collective-permute-start | bytes 294920 | tf_op jit(solution)/shard_map/ppermute | solution.py:25
  117.8 13.0 %collective-permute-start.57 = (bf16[48,1024]{1,0:T(8,128)(2,1)S(1)}, bf16[48,1024]{1,0:T(8,128)(2,1)S(1)}, u32[]{:S(2)}, u32[]{:S(2)}) collective-permute-start(bf16[48,1024]{1,0:T(8,128)(2,1)S(1)} %get-tuple-element.104), channel_id=1, source_target_pairs={{0,4},{1,5},{2,6},{3,7},{4,0},{5,1},{6,2},{7,3},{8,12},{9,13},{10,... | collective-permute-start | bytes 294920 | tf_op jit(solution)/shard_map/ppermute | solution.py:25
  117.9 14.5 %collective-permute-start.58 = (bf16[48,1024]{1,0:T(8,128)(2,1)S(1)}, bf16[48,1024]{1,0:T(8,128)(2,1)S(1)}, u32[]{:S(2)}, u32[]{:S(2)}) collective-permute-start(bf16[48,1024]{1,0:T(8,128)(2,1)S(1)} %get-tuple-element.105), channel_id=1, source_target_pairs={{0,5},{1,4},{2,7},{3,6},{4,1},{5,0},{6,3},{7,2},{8,13},{9,12},{10,... | collective-permute-start | bytes 294920 | tf_op jit(solution)/shard_map/ppermute | solution.py:25
  124.6 10.3 %collective-permute-start.56 = (bf16[48,1024]{1,0:T(8,128)(2,1)S(1)}, bf16[48,1024]{1,0:T(8,128)(2,1)S(1)}, u32[]{:S(2)}, u32[]{:S(2)}) collective-permute-start(bf16[48,1024]{1,0:T(8,128)(2,1)S(1)} %get-tuple-element.103), channel_id=1, source_target_pairs={{0,3},{1,2},{2,1},{3,0},{4,7},{5,6},{6,5},{7,4},{8,11},{9,10},{10,... | collective-permute-start | bytes 294920 | tf_op jit(solution)/shard_map/ppermute | solution.py:25
  (44 other events, 453.1 us)
